TPU v7x, 32 devices: a whole 2x2x4 slice. The times are simulated.
32 devices in a mesh: seq: 16 (over z, y, x), heads: 2 (over core).
Axes of the slice: x: 2, y: 2, z: 4, core: 2. Of those that a mesh axis runs over, the one named last changes fastest.
Arguments:
- hidden_in: bfloat16 [8192, 768], P('seq'), may hold values from -6 to 6
- memory: bfloat16 [8192, 768], P('seq'), may hold values from -6 to 6
- out_grad: bfloat16 [8192, 768], P('seq'), may hold values from -6 to 6
- norm_self: float32 [768], P('seq'), may hold values from 0.5 to 1.5
- self_q: float32 [768, 768], P('seq', 'heads'), may hold values from -0.4375 to 0.4375
- self_k: float32 [768, 768], P('seq', 'heads'), may hold values from -0.21875 to 0.21875
- self_v: float32 [768, 768], P('seq', 'heads'), may hold values from -0.21875 to 0.21875
- self_o: float32 [768, 768], P('heads', 'seq'), may hold values from -0.875 to 0.875
- norm_cross: float32 [768], P('seq'), may hold values from 0.5 to 1.5
- cross_q: float32 [768, 768], P('seq', 'heads'), may hold values from -0.4375 to 0.4375
- cross_k: float32 [768, 768], P('seq', 'heads'), may hold values from -0.21875 to 0.21875
- cross_v: float32 [768, 768], P('seq', 'heads'), may hold values from -0.21875 to 0.21875
- cross_o: float32 [768, 768], P('heads', 'seq'), may hold values from -0.875 to 0.875
- norm_ff: float32 [768], P('seq'), may hold values from 0.5 to 1.5
- ff_in: float32 [768, 3072], P('seq', 'heads'), may hold values from -0.21875 to 0.21875
- ff_out: float32 [3072, 768], P('heads', 'seq'), may hold values from -0.15625 to 0.15625
- bias_table: float32 [32, 12], P(None, 'heads'), may hold values from -4 to 4
- seg_ids: int32 [8192], replicated, may hold values from 0 to 32, as said below
- mem_seg: int32 [8192], replicated, may hold values from -1 to 32, as said below
- rel_bucket: int32 [1024], replicated, may hold values from 0 to 31, as said below
Outputs:
- mixed: bfloat16 [8192, 768], P('seq')
- grad_hidden: float32 [8192, 768], P('seq')
- grad_memory: float32 [8192, 768], P('seq')
- grad_norm_self: float32 [768], P('seq')
- grad_self_q: float32 [768, 768], P('seq', 'heads')
- grad_self_k: float32 [768, 768], P('seq', 'heads')
- grad_self_v: float32 [768, 768], P('seq', 'heads')
- grad_self_o: float32 [768, 768], P('heads', 'seq')
- grad_norm_cross: float32 [768], P('seq')
- grad_cross_q: float32 [768, 768], P('seq', 'heads')
- grad_cross_k: float32 [768, 768], P('seq', 'heads')
- grad_cross_v: float32 [768, 768], P('seq', 'heads')
- grad_cross_o: float32 [768, 768], P('heads', 'seq')
- grad_norm_ff: float32 [768], P('seq')
- grad_ff_in: float32 [768, 3072], P('seq', 'heads')
- grad_ff_out: float32 [3072, 768], P('heads', 'seq')
- grad_bias_table: float32 [32, 12], P(None, 'heads')
Inputs may be any that keep to these rules, and one draw needn't show every extreme that they name: `seg_ids`: segment ids start at 0 and rise by 0 or 1 from one token to the next; they never rise at the first token of an aligned block of 512 tokens and rise 1 to 3 times inside each such block, so every segment lies in two neighbouring blocks. `mem_seg`: memory block k (the k-th aligned block of 512 tokens) holds a live prefix, then padding (-1); its live tokens carry, in order, the ids of the segments whose first token lies in target block k, each such segment one or more tokens. Some block is live throughout. rel_bucket[d] = d for d < 16; after that it never falls and rises by at most 1 from one distance to the next, reaching 31.
All inputs are finite; a program needn't handle non-finite values.
Results may differ from a plain program's by a relative error of at most 0.025.
The roundings to bfloat16 on the way count: a program that leaves them out, or rounds other values in their place, can miss the bound.
Values may be sent and summed in bfloat16 or wider, within the bound.
No kernel may reach another device: no remote copies, remote signals or barrier semaphores. Data moves between devices by JAX's collectives and lax.ppermute only.
A program may use at most 128 MiB of HBM per device.

v0:
```python
import jax
import jax.numpy as jnp
from jax import lax
from jax.sharding import PartitionSpec as P

EPSILON = 1e-06
MASKED = -1000000000.0


def shifted(value, axis, steps):
    count = lax.axis_size(axis)
    leading, last = (max(0, -steps), min(count, count - steps))
    return lax.ppermute(value, axis, [(source, source + steps) for source in range(leading, last)])


def rms_scale(values):
    return values * lax.rsqrt(jnp.mean(values * values, axis=-1, keepdims=True) + EPSILON)


def norm_apply(values, gain):
    return rms_scale(values) * gain


def matmul(spec, left, right):
    return jnp.einsum(spec, left, right, preferred_element_type=jnp.float32)


def split_heads(values, local_heads):
    return values.reshape(values.shape[0], local_heads, values.shape[1] // local_heads)


def merge_heads(values):
    return values.reshape(values.shape[0], values.shape[1] * values.shape[2])


def head_sum(values):
    return lax.psum(values, "heads")


def masked_scores(queries, keys, allowed, rel_bias, factor):
    scores = matmul("ihd,jhd->hij", queries, keys) * factor + rel_bias
    return jnp.where(allowed[None], scores, MASKED)


def attend_forward(queries, keys, values, allowed, rel_bias, factor):
    scores = masked_scores(queries, keys, allowed, rel_bias, factor)
    peak = jnp.max(scores, axis=-1, keepdims=True)
    raised = jnp.exp(scores - peak)
    totals = jnp.sum(raised, axis=-1, keepdims=True)
    weights = (raised / totals).astype(jnp.bfloat16)
    return (matmul("hij,jhd->ihd", weights, values), peak + jnp.log(totals))


def attend_backward(queries, keys, values, allowed, rel_bias, logsum, grad_out, factor):
    weights = jnp.exp(masked_scores(queries, keys, allowed, rel_bias, factor) - logsum)
    grad_weights = matmul("ihd,jhd->hij", grad_out, values)
    inner = jnp.sum(weights * grad_weights, axis=-1, keepdims=True)
    grad_scores = (weights * (grad_weights - inner)).astype(jnp.bfloat16)
    grad_queries = matmul("hij,jhd->ihd", grad_scores, keys) * factor
    grad_keys = matmul("hij,ihd->jhd", grad_scores, queries) * factor
    grad_values = matmul("hij,ihd->jhd", weights.astype(jnp.bfloat16), grad_out)
    return (grad_queries, grad_keys, grad_values, grad_scores)


def per_device(
    hidden_in,
    memory,
    out_grad,
    norm_self,
    self_q,
    self_k,
    self_v,
    self_o,
    norm_cross,
    cross_q,
    cross_k,
    cross_v,
    cross_o,
    norm_ff,
    ff_in,
    ff_out,
    bias_table,
    seg_ids,
    mem_seg,
    rel_bucket,
):
    low_type = jnp.bfloat16
    (
        gain_self,
        query_self,
        key_self,
        value_self,
        out_self,
        gain_cross,
        query_cross,
        key_cross,
        value_cross,
        out_cross,
        gain_ff,
        ff_up,
        ff_down,
    ) = (
        lax.all_gather(norm_self.astype(low_type), "seq", axis=0, tiled=True),
        lax.all_gather(self_q.astype(low_type), "seq", axis=0, tiled=True),
        lax.all_gather(self_k.astype(low_type), "seq", axis=0, tiled=True),
        lax.all_gather(self_v.astype(low_type), "seq", axis=0, tiled=True),
        lax.all_gather(self_o.astype(low_type), "seq", axis=1, tiled=True),
        lax.all_gather(norm_cross.astype(low_type), "seq", axis=0, tiled=True),
        lax.all_gather(cross_q.astype(low_type), "seq", axis=0, tiled=True),
        lax.all_gather(cross_k.astype(low_type), "seq", axis=0, tiled=True),
        lax.all_gather(cross_v.astype(low_type), "seq", axis=0, tiled=True),
        lax.all_gather(cross_o.astype(low_type), "seq", axis=1, tiled=True),
        lax.all_gather(norm_ff.astype(low_type), "seq", axis=0, tiled=True),
        lax.all_gather(ff_in.astype(low_type), "seq", axis=0, tiled=True),
        lax.all_gather(ff_out.astype(low_type), "seq", axis=1, tiled=True),
    )
    row_count = hidden_in.shape[0]
    mem_count = memory.shape[0]
    local_heads = bias_table.shape[1]
    local_width = self_q.shape[1]
    bucket_count = bias_table.shape[0]
    factor = (local_width // local_heads) ** (-0.5)
    position = lax.axis_index("seq")
    earlier = position > 0
    seg_own = lax.dynamic_slice_in_dim(seg_ids, position * row_count, row_count)
    seg_before = lax.dynamic_slice_in_dim(
        seg_ids, jnp.maximum(position - 1, 0) * row_count, row_count
    )
    mem_own = lax.dynamic_slice_in_dim(mem_seg, position * mem_count, mem_count)
    mem_before = lax.dynamic_slice_in_dim(
        mem_seg, jnp.maximum(position - 1, 0) * mem_count, mem_count
    )
    seg_keys = jnp.concatenate([seg_before, seg_own])
    mem_keys = jnp.concatenate([mem_before, mem_own])
    query_index = jnp.arange(row_count, dtype=jnp.int32)[:, None]
    key_index = jnp.arange(2 * row_count, dtype=jnp.int32)[None, :]
    distance = query_index + row_count - key_index
    self_allowed = (
        (seg_own[:, None] == seg_keys[None, :])
        & (distance >= 0)
        & (earlier | (key_index >= row_count))
    )
    mem_index = jnp.arange(2 * mem_count, dtype=jnp.int32)[None, :]
    cross_allowed = (seg_own[:, None] == mem_keys[None, :]) & (earlier | (mem_index >= mem_count))
    bucket_edges = jnp.sum(
        (rel_bucket[:, None] < jnp.arange(bucket_count + 1, dtype=jnp.int32)[None, :]).astype(
            jnp.int32
        ),
        axis=0,
    )
    pair_table = (distance[:, :, None] >= bucket_edges[None, None, :-1]) & (
        distance[:, :, None] < bucket_edges[None, None, 1:]
    )
    rel_bias = jnp.einsum(
        "ijb,bh->hij", pair_table.astype(jnp.float32), bias_table, precision=lax.Precision.HIGHEST
    )
    stream_in = hidden_in.astype(jnp.float32)
    normed_one = norm_apply(stream_in, gain_self.astype(jnp.float32)).astype(low_type)
    query_one = matmul("td,dw->tw", normed_one, query_self).astype(low_type)
    key_one = matmul("td,dw->tw", normed_one, key_self).astype(low_type)
    value_one = matmul("td,dw->tw", normed_one, value_self).astype(low_type)
    mem_key = matmul("md,dw->mw", memory, key_cross).astype(low_type)
    mem_value = matmul("md,dw->mw", memory, value_cross).astype(low_type)
    before = shifted((key_one, value_one, mem_key, mem_value), "seq", 1)
    keys_self = split_heads(jnp.concatenate([before[0], key_one]), local_heads)
    values_self = split_heads(jnp.concatenate([before[1], value_one]), local_heads)
    keys_mem = split_heads(jnp.concatenate([before[2], mem_key]), local_heads)
    values_mem = split_heads(jnp.concatenate([before[3], mem_value]), local_heads)
    queries_one = split_heads(query_one, local_heads)
    attended_one, logsum_one = attend_forward(
        queries_one, keys_self, values_self, self_allowed, rel_bias, factor
    )
    attend_one = merge_heads(attended_one).astype(low_type)
    stream_one = stream_in + head_sum(matmul("tw,wd->td", attend_one, out_self))
    normed_two = norm_apply(stream_one, gain_cross.astype(jnp.float32)).astype(low_type)
    query_two = matmul("td,dw->tw", normed_two, query_cross).astype(low_type)
    queries_two = split_heads(query_two, local_heads)
    attended_two, logsum_two = attend_forward(
        queries_two, keys_mem, values_mem, cross_allowed, 0.0, factor
    )
    attend_two = merge_heads(attended_two).astype(low_type)
    stream_two = stream_one + head_sum(matmul("tw,wd->td", attend_two, out_cross))
    normed_three = norm_apply(stream_two, gain_ff.astype(jnp.float32)).astype(low_type)
    hidden_pre = matmul("td,df->tf", normed_three, ff_up)
    active = jax.nn.gelu(hidden_pre).astype(low_type)
    stream_out = stream_two + head_sum(matmul("tf,fd->td", active, ff_down))
    mixed = stream_out.astype(low_type)
    grad_out = out_grad.astype(jnp.float32)
    grad_down = matmul("tf,td->fd", active, out_grad)
    grad_active = matmul("td,fd->tf", out_grad, ff_down)
    gelu_value, gelu_pull = jax.vjp(jax.nn.gelu, hidden_pre)
    grad_pre = gelu_pull(grad_active)[0].astype(low_type)
    grad_up = matmul("td,tf->df", normed_three, grad_pre)
    grad_normed_three = head_sum(matmul("tf,df->td", grad_pre, ff_up))
    norm_value, norm_pull = jax.vjp(norm_apply, stream_two, gain_ff.astype(jnp.float32))
    grad_stream_three, grad_gain_ff = norm_pull(grad_normed_three)
    grad_two = grad_out + grad_stream_three
    ff_summed = (
        lax.psum_scatter(grad_gain_ff, "seq", scatter_dimension=0, tiled=True),
        lax.psum_scatter(grad_up, "seq", scatter_dimension=0, tiled=True),
        lax.psum_scatter(grad_down, "seq", scatter_dimension=1, tiled=True),
    )
    low_two = grad_two.astype(low_type)
    grad_out_cross = matmul("tw,td->wd", attend_two, low_two)
    grad_attend_two = split_heads(
        matmul("td,wd->tw", low_two, out_cross).astype(low_type), local_heads
    )
    grad_queries_two, grad_mem_keys, grad_mem_values, unused_scores = attend_backward(
        queries_two, keys_mem, values_mem, cross_allowed, 0.0, logsum_two, grad_attend_two, factor
    )
    grad_query_two = merge_heads(grad_queries_two).astype(low_type)
    grad_query_cross = matmul("td,tw->dw", normed_two, grad_query_two)
    grad_normed_two = head_sum(matmul("tw,dw->td", grad_query_two, query_cross))
    norm_value, norm_pull = jax.vjp(norm_apply, stream_one, gain_cross.astype(jnp.float32))
    grad_stream_two, grad_gain_cross = norm_pull(grad_normed_two)
    grad_one = grad_two + grad_stream_two
    cross_summed = (
        lax.psum_scatter(grad_gain_cross, "seq", scatter_dimension=0, tiled=True),
        lax.psum_scatter(grad_query_cross, "seq", scatter_dimension=0, tiled=True),
        lax.psum_scatter(grad_out_cross, "seq", scatter_dimension=1, tiled=True),
    )
    low_one = grad_one.astype(low_type)
    grad_out_self = matmul("tw,td->wd", attend_one, low_one)
    grad_attend_one = split_heads(
        matmul("td,wd->tw", low_one, out_self).astype(low_type), local_heads
    )
    grad_queries_one, grad_keys_self, grad_values_self, grad_scores = attend_backward(
        queries_one,
        keys_self,
        values_self,
        self_allowed,
        rel_bias,
        logsum_one,
        grad_attend_one,
        factor,
    )
    grad_table_part = matmul("hij,ijb->bh", grad_scores, pair_table.astype(low_type))
    flat_keys = merge_heads(grad_keys_self)
    flat_values = merge_heads(grad_values_self)
    flat_mem_keys = merge_heads(grad_mem_keys)
    flat_mem_values = merge_heads(grad_mem_values)
    later = (
        shifted(flat_keys[:row_count].astype(jnp.bfloat16), "seq", -1).astype(jnp.float32),
        shifted(flat_values[:row_count].astype(jnp.bfloat16), "seq", -1).astype(jnp.float32),
        shifted(flat_mem_keys[:mem_count].astype(jnp.bfloat16), "seq", -1).astype(jnp.float32),
        shifted(flat_mem_values[:mem_count].astype(jnp.bfloat16), "seq", -1).astype(jnp.float32),
    )
    grad_key_one = (flat_keys[row_count:] + later[0]).astype(low_type)
    grad_value_one = (flat_values[row_count:] + later[1]).astype(low_type)
    grad_mem_key = (flat_mem_keys[mem_count:] + later[2]).astype(low_type)
    grad_mem_value = (flat_mem_values[mem_count:] + later[3]).astype(low_type)
    grad_query_one = merge_heads(grad_queries_one).astype(low_type)
    grad_query_self = matmul("td,tw->dw", normed_one, grad_query_one)
    grad_key_self = matmul("td,tw->dw", normed_one, grad_key_one)
    grad_value_self = matmul("td,tw->dw", normed_one, grad_value_one)
    grad_key_cross = matmul("md,mw->dw", memory, grad_mem_key)
    grad_value_cross = matmul("md,mw->dw", memory, grad_mem_value)
    normed_part = (
        matmul("tw,dw->td", grad_query_one, query_self)
        + matmul("tw,dw->td", grad_key_one, key_self)
        + matmul("tw,dw->td", grad_value_one, value_self)
    )
    memory_part = matmul("mw,dw->md", grad_mem_key, key_cross) + matmul(
        "mw,dw->md", grad_mem_value, value_cross
    )
    grad_normed_one, grad_memory = head_sum((normed_part, memory_part))
    norm_value, norm_pull = jax.vjp(norm_apply, stream_in, gain_self.astype(jnp.float32))
    grad_stream_one, grad_gain_self = norm_pull(grad_normed_one)
    grad_hidden = grad_one + grad_stream_one
    rest_summed = (
        lax.psum_scatter(grad_gain_self, "seq", scatter_dimension=0, tiled=True),
        lax.psum_scatter(grad_query_self, "seq", scatter_dimension=0, tiled=True),
        lax.psum_scatter(grad_key_self, "seq", scatter_dimension=0, tiled=True),
        lax.psum_scatter(grad_value_self, "seq", scatter_dimension=0, tiled=True),
        lax.psum_scatter(grad_out_self, "seq", scatter_dimension=1, tiled=True),
        lax.psum_scatter(grad_key_cross, "seq", scatter_dimension=0, tiled=True),
        lax.psum_scatter(grad_value_cross, "seq", scatter_dimension=0, tiled=True),
    )
    summed = (
        rest_summed[0],
        rest_summed[1],
        rest_summed[2],
        rest_summed[3],
        rest_summed[4],
        cross_summed[0],
        cross_summed[1],
        rest_summed[5],
        rest_summed[6],
        cross_summed[2],
        ff_summed[0],
        ff_summed[1],
        ff_summed[2],
    )
    grad_table = lax.psum(grad_table_part, "seq")
    return (
        mixed,
        grad_hidden,
        grad_memory,
        summed[0],
        summed[1],
        summed[2],
        summed[3],
        summed[4],
        summed[5],
        summed[6],
        summed[7],
        summed[8],
        summed[9],
        summed[10],
        summed[11],
        summed[12],
        grad_table,
    )


def solution(mesh):
    in_specs = (
        P("seq", None),
        P("seq", None),
        P("seq", None),
        P("seq"),
        P("seq", "heads"),
        P("seq", "heads"),
        P("seq", "heads"),
        P("heads", "seq"),
        P("seq"),
        P("seq", "heads"),
        P("seq", "heads"),
        P("seq", "heads"),
        P("heads", "seq"),
        P("seq"),
        P("seq", "heads"),
        P("heads", "seq"),
        P(None, "heads"),
        P(),
        P(),
        P(),
    )
    out_specs = (
        P("seq", None),
        P("seq", None),
        P("seq", None),
        P("seq"),
        P("seq", "heads"),
        P("seq", "heads"),
        P("seq", "heads"),
        P("heads", "seq"),
        P("seq"),
        P("seq", "heads"),
        P("seq", "heads"),
        P("seq", "heads"),
        P("heads", "seq"),
        P("seq"),
        P("seq", "heads"),
        P("heads", "seq"),
        P(None, "heads"),
    )
    return jax.shard_map(
        per_device, mesh=mesh, in_specs=in_specs, out_specs=out_specs, check_vma=False
    )
```

profile of v0, /device:TPU:2, one launch (start us, length us, event | category | flops | bytes accessed | tf_op | source)
XLA Modules:
  0.0 2084.3 jit_solution(18204922821335537356)
XLA Ops:
  14.2 38.0 %all-reduce.8 = (bf16[768]{0:T(1024)(128)(2,1)S(1)}, bf16[768]{0:T(1024)(128)(2,1)S(1)}, bf16[768]{0:T(1024)(128)(2,1)S(1)}) all-reduce(bf16[768]{0:T(1024)(128)(2,1)S(1)} %dynamic-update-slice, bf16[768]{0:T(1024)(128)(2,1)S(1)} %dynamic-update-slice.1, bf16[768]{0:T(1024)(128)(2,1)S(1)} %dynamic-update-slice.2), channel_id=1, replica_groups=mesh['seq'=16,'heads'=2] {'seq'}, use_global_device_ids=true, to_apply=%add | all-reduce | flops 2304 | bytes 9216
  53.1 44.4 %all_gather.40 = bf16[768,384]{1,0:T(8,128)(2,1)S(1)} all-gather(bf16[48,384]{1,0:T(8,128)(2,1)S(1)} %convert_element_type.208), channel_id=1, replica_groups=mesh['seq'=16,'heads'=2] {'seq'}, dimensions={0}, use_global_device_ids=true | all-gather | bytes 626688 | tf_op jit(solution)/shard_map/all_gather | solution.py:106
  100.2 42.8 %all_gather.42 = bf16[768,384]{1,0:T(8,128)(2,1)S(1)} all-gather(bf16[48,384]{1,0:T(8,128)(2,1)S(1)} %convert_element_type.212), channel_id=1, replica_groups=mesh['seq'=16,'heads'=2] {'seq'}, dimensions={0}, use_global_device_ids=true | all-gather | bytes 626688 | tf_op jit(solution)/shard_map/all_gather | solution.py:105
  147.4 43.9 %all_gather.44 = bf16[768,384]{1,0:T(8,128)(2,1)} all-gather(bf16[48,384]{1,0:T(8,128)(2,1)S(1)} %convert_element_type.220), channel_id=1, replica_groups=mesh['seq'=16,'heads'=2] {'seq'}, dimensions={0}, use_global_device_ids=true | all-gather | bytes 626688 | tf_op jit(solution)/shard_map/all_gather | solution.py:111
  191.4 42.7 %all_gather.43 = bf16[384,768]{0,1:T(8,128)(2,1)} all-gather(bf16[384,48]{0,1:T(8,128)(2,1)S(1)} %convert_element_type.219), channel_id=1, replica_groups=mesh['seq'=16,'heads'=2] {'seq'}, dimensions={1}, use_global_device_ids=true | all-gather | bytes 626688 | tf_op jit(solution)/shard_map/all_gather | solution.py:107
  238.3 26.6 %fusion.1 = f32[512,1024,6]{1,2,0:T(8,128)} fusion(s32[512,1024]{1,0:T(8,128)} %iota_subtract_fusion, s32[32]{0:T(128)S(1)} %get-tuple-element.114, s32[32]{0:T(128)S(1)} %get-tuple-element.113, f32[32,6]{0,1:T(8,128)S(1)} %copy-done.101), kind=kOutput, calls=%fused_computation.2 | convolution fusion | flops 1258291200 | bytes 14681088 | tf_op jit(solution)/shard_map/ijb,bh->hij/dot_general | solution.py:154
  264.9 39.5 %all_gather.41 = bf16[768,384]{1,0:T(8,128)(2,1)S(1)} all-gather(bf16[48,384]{1,0:T(8,128)(2,1)S(1)} %convert_element_type.210), channel_id=1, replica_groups=mesh['seq'=16,'heads'=2] {'seq'}, dimensions={0}, use_global_device_ids=true | all-gather | bytes 626688 | tf_op jit(solution)/shard_map/all_gather | solution.py:104
  311.1 14.8 fusion.84
  338.6 41.1 %all_gather.47 = bf16[768,384]{1,0:T(8,128)(2,1)S(1)} all-gather(bf16[48,384]{1,0:T(8,128)(2,1)S(1)} %convert_element_type.227), channel_id=1, replica_groups=mesh['seq'=16,'heads'=2] {'seq'}, dimensions={0}, use_global_device_ids=true | all-gather | bytes 626688 | tf_op jit(solution)/shard_map/all_gather | solution.py:110
  382.2 43.0 %all_gather.48 = bf16[384,768]{0,1:T(8,128)(2,1)} all-gather(bf16[384,48]{0,1:T(8,128)(2,1)S(1)} %convert_element_type.233), channel_id=1, replica_groups=mesh['seq'=16,'heads'=2] {'seq'}, dimensions={1}, use_global_device_ids=true | all-gather | bytes 626688 | tf_op jit(solution)/shard_map/all_gather | solution.py:112
  425.2 43.3 %all_gather.46 = bf16[768,384]{1,0:T(8,128)(2,1)} all-gather(bf16[48,384]{1,0:T(8,128)(2,1)S(1)} %convert_element_type.225), channel_id=1, replica_groups=mesh['seq'=16,'heads'=2] {'seq'}, dimensions={0}, use_global_device_ids=true | all-gather | bytes 626688 | tf_op jit(solution)/shard_map/all_gather | solution.py:109
  490.6 14.6 all-reduce.17.cloned.1.call-done
  508.5 42.2 %all-gather.5.cloned.1.call-done = bf16[1536,768]{0,1:T(8,128)(2,1)} async-done(((bf16[1536,48]{0,1:T(8,128)(2,1)}), bf16[1536,768]{0,1:T(8,128)(2,1)}) %all-gather.5.cloned.1.call-update) | async-done | bytes 2359312 | tf_op jit(solution)/shard_map/all_gather | solution.py:115
  555.7 59.1 %all-gather.3.cloned.1.call-done = bf16[768,1536]{1,0:T(8,128)(2,1)} async-done(((bf16[48,1536]{1,0:T(8,128)(2,1)}), bf16[768,1536]{1,0:T(8,128)(2,1)}) %all-gather.3.cloned.1.call-update) | async-done | bytes 2359312 | tf_op jit(solution)/shard_map/all_gather | solution.py:114
  614.8 7.9 fusion.28
  628.8 16.8 all-reduce.19.cloned.1.call-done
  659.9 6.3 multiply_reduce_fusion.1
  692.9 6.5 collective-permute-done.6
  711.5 6.6 fusion.41
  739.9 7.4 collective-permute-done.4
  748.8 6.3 collective-permute-done.5
  793.0 18.2 fusion.48
  813.3 68.4 %all-reduce.6 = (f32[768]{0:T(1024)S(1)}, f32[768]{0:T(1024)S(1)}, f32[768]{0:T(1024)S(1)}, f32[32,6]{0,1:T(8,128)}) all-reduce(f32[768]{0:T(1024)S(1)} %get-tuple-element.89, f32[768]{0:T(1024)S(1)} %copy-done.94, f32[768]{0:T(1024)S(1)} %copy-done.93, f32[32,6]{0,1:T(8,128)S(1)} %fusion.48), channel_id=2, replica_groups=mesh['seq'=16,'heads'=2] {'seq'}, use_global_device_ids=true, to_apply=%region_21.22.clone | all-reduce | flops 2496 | bytes 19968
  889.1 128.7 %reduce-scatter.23.cloned.1.call-done = f32[48,384]{1,0:T(8,128)} async-done(((f32[768,384]{1,0:T(8,128)}), f32[48,384]{1,0:T(8,128)}) %reduce-scatter.23.cloned.1.call-update) | async-done | bytes 73744 | tf_op jit(solution)/shard_map/reduce_scatter | solution.py:219
  1017.8 128.8 %reduce-scatter.33.cloned.1.call-done = f32[48,384]{1,0:T(8,128)} async-done(((f32[768,384]{1,0:T(8,128)}), f32[48,384]{1,0:T(8,128)}) %reduce-scatter.33.cloned.1.call-update) | async-done | bytes 73744
  1146.6 128.8 %reduce-scatter.31.cloned.1.call-done = f32[48,384]{1,0:T(8,128)} async-done(((f32[768,384]{1,0:T(8,128)}), f32[48,384]{1,0:T(8,128)}) %reduce-scatter.31.cloned.1.call-update) | async-done | bytes 73744
  1275.4 128.7 %reduce-scatter.21.cloned.1.call-done = f32[384,48]{0,1:T(8,128)} async-done(((f32[384,768]{0,1:T(8,128)}), f32[384,48]{0,1:T(8,128)}) %reduce-scatter.21.cloned.1.call-update) | async-done | bytes 73744 | tf_op jit(solution)/shard_map/reduce_scatter | solution.py:275
  1404.2 128.8 %reduce-scatter.15.cloned.1.call-done = f32[48,384]{1,0:T(8,128)} async-done(((f32[768,384]{1,0:T(8,128)}), f32[48,384]{1,0:T(8,128)}) %reduce-scatter.15.cloned.1.call-update) | async-done | bytes 73744 | tf_op jit(solution)/shard_map/reduce_scatter | solution.py:272
  1532.9 128.8 %reduce-scatter.19.cloned.1.call-done = f32[48,384]{1,0:T(8,128)} async-done(((f32[768,384]{1,0:T(8,128)}), f32[48,384]{1,0:T(8,128)}) %reduce-scatter.19.cloned.1.call-update) | async-done | bytes 73744 | tf_op jit(solution)/shard_map/reduce_scatter | solution.py:274
  1661.7 128.8 %reduce-scatter.17.cloned.1.call-done = f32[48,384]{1,0:T(8,128)} async-done(((f32[768,384]{1,0:T(8,128)}), f32[48,384]{1,0:T(8,128)}) %reduce-scatter.17.cloned.1.call-update) | async-done | bytes 73744 | tf_op jit(solution)/shard_map/reduce_scatter | solution.py:273
  1790.6 143.0 %reduce-scatter.29.cloned.1.call-done = f32[1536,48]{0,1:T(8,128)} async-done(((f32[1536,768]{0,1:T(8,128)}), f32[1536,48]{0,1:T(8,128)}) %reduce-scatter.29.cloned.1.call-update) | async-done | bytes 294928 | tf_op jit(solution)/shard_map/reduce_scatter | solution.py:201
  1933.6 141.9 %reduce-scatter.27.cloned.1.call-done = f32[48,1536]{1,0:T(8,128)} async-done(((f32[768,1536]{1,0:T(8,128)}), f32[48,1536]{1,0:T(8,128)}) %reduce-scatter.27.cloned.1.call-update) | async-done | bytes 294928 | tf_op jit(solution)/shard_map/reduce_scatter | solution.py:200
  (391 shorter events, 198.8 us)
Async XLA Ops:
  8.0 327.9 %copy-start = (bf16[512,768]{1,0:T(8,128)(2,1)S(1)}, bf16[512,768]{1,0:T(8,128)(2,1)}, u32[]{:S(2)}) copy-start(bf16[512,768]{1,0:T(8,128)(2,1)} %param.21) | copy-start | bytes 2359300
  8.0 463.0 %all-reduce.15.cloned.1.call-start = ((), (), s32[]{:S(2)}) async-start(), calls=%async_computation.10 | async-start | bytes 3145728 | tf_op jit(solution)/shard_map/psum | solution.py:37
  11.6 292.8 %copy-start.79 = (f32[512]{0:T(512)}, f32[512]{0:T(512)S(1)}, u32[]{:S(2)}) copy-start(f32[512]{0:T(512)S(1)} %fusion.63) | copy-start | bytes 6148
  52.2 252.2 %copy-start.66 = (f32[768]{0:T(1024)}, f32[768]{0:T(1024)S(1)}, u32[]{:S(2)}) copy-start(f32[768]{0:T(1024)S(1)} %convert_element_type.206) | copy-start | bytes 9220
  98.2 207.0 %collective-permute-start = (bf16[512,384]{1,0:T(8,128)(2,1)S(1)}, bf16[512,384]{1,0:T(8,128)(2,1)}, u32[]{:S(2)}, u32[]{:S(2)}) collective-permute-start(bf16[512,384]{1,0:T(8,128)(2,1)S(1)} %convolution_convert_fusion.7), channel_id=1, source_target_pairs={{0,2},{2,4},{4,6},{6,8},{8,10},{10,12},{12,14},{14,16},{16,18},{18... | collective-permute-start | bytes 1179656 | tf_op jit(solution)/shard_map/ppermute | solution.py:13
  145.2 162.4 %collective-permute-start.1 = (bf16[512,384]{1,0:T(8,128)(2,1)}, bf16[512,384]{1,0:T(8,128)(2,1)}, u32[]{:S(2)}, u32[]{:S(2)}) collective-permute-start(bf16[512,384]{1,0:T(8,128)(2,1)} %convolution_convert_fusion.5), channel_id=1, source_target_pairs={{0,2},{2,4},{4,6},{6,8},{8,10},{10,12},{12,14},{14,16},{16,18},{18... | collective-permute-start | bytes 1179656 | tf_op jit(solution)/shard_map/ppermute | solution.py:13
  147.4 90.9 %copy-start.98 = (s32[32]{0:T(128)}, s32[32]{0:T(128)S(1)}, u32[]{:S(2)}) copy-start(s32[32]{0:T(128)S(1)} %get-tuple-element.114) | copy-start | bytes 388
  335.8 169.4 %all-reduce.17.cloned.1.call-start = ((), (), s32[]{:S(2)}) async-start(), calls=%async_computation.11 | async-start | bytes 3145728 | tf_op jit(solution)/shard_map/psum | solution.py:37
  336.5 132.0 %collective-permute-start.2 = (bf16[512,384]{1,0:T(8,128)(2,1)S(1)}, bf16[512,384]{1,0:T(8,128)(2,1)S(1)}, u32[]{:S(2)}, u32[]{:S(2)}) collective-permute-start(bf16[512,384]{1,0:T(8,128)(2,1)S(1)} %convolution_convert_fusion.4), channel_id=1, source_target_pairs={{0,2},{2,4},{4,6},{6,8},{8,10},{10,12},{12,14},{14,16},{16,18},{18... | collective-permute-start | bytes 1179656 | tf_op jit(solution)/shard_map/ppermute | solution.py:13
  380.2 89.5 %collective-permute-start.3 = (bf16[512,384]{1,0:T(8,128)(2,1)S(1)}, bf16[512,384]{1,0:T(8,128)(2,1)S(1)}, u32[]{:S(2)}, u32[]{:S(2)}) collective-permute-start(bf16[512,384]{1,0:T(8,128)(2,1)S(1)} %convolution_convert_fusion.2), channel_id=1, source_target_pairs={{0,2},{2,4},{4,6},{6,8},{8,10},{10,12},{12,14},{14,16},{16,18},{18... | collective-permute-start | bytes 1179656 | tf_op jit(solution)/shard_map/ppermute | solution.py:13
  487.1 63.6 %all-gather.5.cloned.1.call-start = ((), (), s32[]{:S(2)}) async-start(), calls=%async_computation.13 | async-start | bytes 2506752 | tf_op jit(solution)/shard_map/all_gather | solution.py:115
  488.9 126.0 %all-gather.3.cloned.1.call-start = ((), (), s32[]{:S(2)}) async-start(), calls=%async_computation.12 | async-start | bytes 2506752 | tf_op jit(solution)/shard_map/all_gather | solution.py:114
  490.6 155.0 %all-reduce.19.cloned.1.call-start = ((), (), s32[]{:S(2)}) async-start(), calls=%async_computation.14 | async-start | bytes 3145728 | tf_op jit(solution)/shard_map/psum | solution.py:37
  490.6 124.2 %copy-start.63 = (f32[768]{0:T(1024)}, f32[768]{0:T(1024)S(1)}, u32[]{:S(2)}) copy-start(f32[768]{0:T(1024)S(1)} %convert_element_type.235) | copy-start | bytes 9220
  508.5 106.3 %copy-start.83 = (f32[512]{0:T(512)}, f32[512]{0:T(512)S(1)}, u32[]{:S(2)}) copy-start(f32[512]{0:T(512)S(1)} %fusion.65) | copy-start | bytes 6148
  626.5 80.3 %all-reduce.21.cloned.1.call-start = ((), (), s32[]{:S(2)}) async-start(), calls=%async_computation.15 | async-start | bytes 3145728 | tf_op jit(solution)/shard_map/psum | solution.py:37
  676.6 15.0 collective-permute-start.7
  678.9 20.6 collective-permute-start.6
  682.6 128.6 %all-reduce.23.cloned.1.call-start = ((), (), s32[]{:S(2)}) async-start(), calls=%async_computation.26 | async-start | bytes 9437184 | tf_op jit(solution)/shard_map/psum | solution.py:37
  732.6 14.7 collective-permute-start.4
  737.0 18.2 collective-permute-start.5
  757.8 131.3 %reduce-scatter.25.cloned.1.call-start = ((), (), s32[]{:S(2)}) async-start(), calls=%async_computation.21 | async-start | bytes 1253376 | tf_op jit(solution)/shard_map/reduce_scatter | solution.py:220
  761.2 256.6 %reduce-scatter.23.cloned.1.call-start = ((), (), s32[]{:S(2)}) async-start(), calls=%async_computation.20 | async-start | bytes 1253376 | tf_op jit(solution)/shard_map/reduce_scatter | solution.py:219
  763.1 383.5 %reduce-scatter.33.cloned.1.call-start = ((), (), s32[]{:S(2)}) async-start(), calls=%async_computation.25 | async-start | bytes 1253376
  766.1 509.3 %reduce-scatter.31.cloned.1.call-start = ((), (), s32[]{:S(2)}) async-start(), calls=%async_computation.24 | async-start | bytes 1253376
  770.9 633.3 %reduce-scatter.21.cloned.1.call-start = ((), (), s32[]{:S(2)}) async-start(), calls=%async_computation.19 | async-start | bytes 1253376 | tf_op jit(solution)/shard_map/reduce_scatter | solution.py:275
  773.7 759.2 %reduce-scatter.15.cloned.1.call-start = ((), (), s32[]{:S(2)}) async-start(), calls=%async_computation.16 | async-start | bytes 1253376 | tf_op jit(solution)/shard_map/reduce_scatter | solution.py:272
  775.6 886.1 %reduce-scatter.19.cloned.1.call-start = ((), (), s32[]{:S(2)}) async-start(), calls=%async_computation.18 | async-start | bytes 1253376 | tf_op jit(solution)/shard_map/reduce_scatter | solution.py:274
  777.5 1013.1 %reduce-scatter.17.cloned.1.call-start = ((), (), s32[]{:S(2)}) async-start(), calls=%async_computation.17 | async-start | bytes 1253376 | tf_op jit(solution)/shard_map/reduce_scatter | solution.py:273
  779.4 1154.2 %reduce-scatter.29.cloned.1.call-start = ((), (), s32[]{:S(2)}) async-start(), calls=%async_computation.23 | async-start | bytes 5013504 | tf_op jit(solution)/shard_map/reduce_scatter | solution.py:201
  785.7 1289.8 %reduce-scatter.27.cloned.1.call-start = ((), (), s32[]{:S(2)}) async-start(), calls=%async_computation.22 | async-start | bytes 5013504 | tf_op jit(solution)/shard_map/reduce_scatter | solution.py:200
  886.1 1189.4 %copy-start.58 = (f32[512,768]{1,0:T(8,128)S(1)}, f32[512,768]{1,0:T(8,128)}, u32[]{:S(2)}) copy-start(f32[512,768]{1,0:T(8,128)} %get-tuple-element.129) | copy-start | bytes 4718596
  (105 other events, 1281.6 us)
Sparse Core Ops, SparseCore 0:
  335.9 18.6 all-reduce.14
  487.3 17.8 all-reduce.16
  626.6 18.9 all-reduce.18
  682.7 24.0 all-reduce.20
  757.9 30.5 all-reduce.22
Sparse Core Ops, SparseCore 1:
  491.0 59.7 all-gather.4
  554.0 60.8 all-gather.2
  764.3 124.7 reduce-scatter.24
  895.1 122.6 reduce-scatter.22
  1023.9 122.7 reduce-scatter.32
  1152.7 122.7 reduce-scatter.30
  1281.3 122.8 reduce-scatter.20
  1410.1 122.8 reduce-scatter.14
  1538.9 122.8 reduce-scatter.18
  1667.8 122.7 reduce-scatter.16
  1797.0 136.5 reduce-scatter.28
  1939.4 136.1 reduce-scatter.26
where the time goes:
time: 2090 us; the launch traced here: 2080 us
  waiting for transfers between devices  1350 us (65%)
  blocking collectives  447 us (21%)
  matrix products  165 us (8%)
  other arithmetic  57.6 us (3%)
  local copies, waits for them, and re-layouts  30.9 us (1%)
    unnamed x19, waiting for transfers between devices  258 us
    reduce_scatter x1, waiting for transfers between devices, per_device(): lax.psum_scatter(grad_down, 'seq', scatter_dimension=1, tiled=True)  143 us
    reduce_scatter x1, waiting for transfers between devices, per_device(): lax.psum_scatter(grad_up, 'seq', scatter_dimension=0, tiled=True)  142 us
    dot_general x43, matrix products, matmul(): return jnp.einsum(spec, left, right, preferred_element_type=jnp.float32)  138 us
    reduce_scatter x1, waiting for transfers between devices, per_device(): lax.psum_scatter(grad_key_self, 'seq', scatter_dimension=0, tiled=True)  129 us
    reduce_scatter x1, waiting for transfers between devices, per_device(): lax.psum_scatter(grad_value_self, 'seq', scatter_dimension=0, tiled=True)  129 us
    reduce_scatter x1, waiting for transfers between devices, per_device(): lax.psum_scatter(grad_query_self, 'seq', scatter_dimension=0, tiled=True)  129 us
    reduce_scatter x1, waiting for transfers between devices, per_device(): lax.psum_scatter(grad_out_self, 'seq', scatter_dimension=1, tiled=True)  129 us
  transfers between devices with their start and end apart: 25, of which 19 were waited for; matrix products, arithmetic and copies ran while one was open for 6% of the time, Pallas kernels for 0%

commit v1 on v0

--- a/solution.py
+++ b/solution.py
@@ -34,7 +34,8 @@
 
 
 def head_sum(values):
-    return lax.psum(values, "heads")
+    other = lax.ppermute(values, "heads", [(0, 1), (1, 0)])
+    return jax.tree.map(jnp.add, values, other)
 
 
 def masked_scores(queries, keys, allowed, rel_bias, factor):
@@ -60,6 +61,69 @@
     grad_keys = matmul("hij,ihd->jhd", grad_scores, queries) * factor
     grad_values = matmul("hij,ihd->jhd", weights.astype(jnp.bfloat16), grad_out)
     return (grad_queries, grad_keys, grad_values, grad_scores)
+
+
+def axis_bits(axis):
+    return lax.axis_size(axis).bit_length() - 1
+
+
+def bit_orders(bits):
+    high = list(range(bits - 1, 1, -1))
+    low = list(range(min(bits, 2)))
+    return high + low[::-1], high + low
+
+
+def partner_swap(value, axis, bit):
+    count = lax.axis_size(axis)
+    return lax.ppermute(value, axis, [(i, i ^ (1 << bit)) for i in range(count)])
+
+
+def my_bit(axis, bit):
+    return (lax.axis_index(axis) >> bit) & 1
+
+
+def gather_rows(shard, axis):
+    bits = axis_bits(axis)
+    cut = shard.shape[1] // 256 * 128
+    halves = []
+    for order, part in zip(bit_orders(bits), (shard[:, :cut], shard[:, cut:])):
+        done = []
+        value = part
+        for bit in order:
+            other = partner_swap(value, axis, bit)
+            place = sum(1 for b in done if b > bit)
+            mine = my_bit(axis, bit) == 0
+            value = jnp.stack(
+                [jnp.where(mine, value, other), jnp.where(mine, other, value)], axis=place
+            )
+            done.append(bit)
+        halves.append(value.reshape(-1, part.shape[1]))
+    return jnp.concatenate(halves, axis=1)
+
+
+def scatter_rows(full, axis):
+    bits = axis_bits(axis)
+    cut = full.shape[1] // 256 * 128
+    halves = []
+    for order, part in zip(bit_orders(bits), (full[:, :cut], full[:, cut:])):
+        value = part.reshape((2,) * bits + (-1, part.shape[1]))
+        left = list(range(bits - 1, -1, -1))
+        for bit in order[::-1]:
+            place = left.index(bit)
+            mine = my_bit(axis, bit)
+            keep = lax.dynamic_index_in_dim(value, mine, place, keepdims=False)
+            send = lax.dynamic_index_in_dim(value, 1 - mine, place, keepdims=False)
+            got = partner_swap(send.astype(jnp.bfloat16), axis, bit)
+            value = keep + got.astype(jnp.float32)
+            left.remove(bit)
+        halves.append(value)
+    return jnp.concatenate(halves, axis=1)
+
+
+def sum_all(value, axis):
+    for bit in range(axis_bits(axis)):
+        value = value + partner_swap(value, axis, bit)
+    return value
 
 
 def per_device(
@@ -85,35 +149,23 @@
     rel_bucket,
 ):
     low_type = jnp.bfloat16
-    (
-        gain_self,
-        query_self,
-        key_self,
-        value_self,
-        out_self,
-        gain_cross,
-        query_cross,
-        key_cross,
-        value_cross,
-        out_cross,
-        gain_ff,
-        ff_up,
-        ff_down,
-    ) = (
-        lax.all_gather(norm_self.astype(low_type), "seq", axis=0, tiled=True),
-        lax.all_gather(self_q.astype(low_type), "seq", axis=0, tiled=True),
-        lax.all_gather(self_k.astype(low_type), "seq", axis=0, tiled=True),
-        lax.all_gather(self_v.astype(low_type), "seq", axis=0, tiled=True),
-        lax.all_gather(self_o.astype(low_type), "seq", axis=1, tiled=True),
-        lax.all_gather(norm_cross.astype(low_type), "seq", axis=0, tiled=True),
-        lax.all_gather(cross_q.astype(low_type), "seq", axis=0, tiled=True),
-        lax.all_gather(cross_k.astype(low_type), "seq", axis=0, tiled=True),
-        lax.all_gather(cross_v.astype(low_type), "seq", axis=0, tiled=True),
-        lax.all_gather(cross_o.astype(low_type), "seq", axis=1, tiled=True),
-        lax.all_gather(norm_ff.astype(low_type), "seq", axis=0, tiled=True),
-        lax.all_gather(ff_in.astype(low_type), "seq", axis=0, tiled=True),
-        lax.all_gather(ff_out.astype(low_type), "seq", axis=1, tiled=True),
-    )
+    part = self_q.shape[1]
+    wide = ff_in.shape[1]
+    gains = jnp.pad(jnp.stack([norm_self, norm_cross, norm_ff], axis=1), ((0, 0), (0, 125)))
+    first = gather_rows(
+        jnp.concatenate([gains, self_q, self_k, self_v], axis=1).astype(low_type), "seq"
+    )
+    second = gather_rows(
+        jnp.concatenate([cross_k, cross_v, self_o.T, cross_q, cross_o.T], axis=1).astype(low_type),
+        "seq",
+    )
+    third = gather_rows(jnp.concatenate([ff_in, ff_out.T], axis=1).astype(low_type), "seq")
+    gain_self, gain_cross, gain_ff = first[:, 0], first[:, 1], first[:, 2]
+    query_self, key_self, value_self = (first[:, 128 + i * part : 128 + (i + 1) * part] for i in range(3))
+    key_cross, value_cross, out_self, query_cross, out_cross = (
+        second[:, i * part : (i + 1) * part] for i in range(5)
+    )
+    ff_up, ff_down = third[:, :wide], third[:, wide:]
     row_count = hidden_in.shape[0]
     mem_count = memory.shape[0]
     local_heads = bias_table.shape[1]
@@ -171,7 +223,7 @@
         queries_one, keys_self, values_self, self_allowed, rel_bias, factor
     )
     attend_one = merge_heads(attended_one).astype(low_type)
-    stream_one = stream_in + head_sum(matmul("tw,wd->td", attend_one, out_self))
+    stream_one = stream_in + head_sum(matmul("tw,dw->td", attend_one, out_self))
     normed_two = norm_apply(stream_one, gain_cross.astype(jnp.float32)).astype(low_type)
     query_two = matmul("td,dw->tw", normed_two, query_cross).astype(low_type)
     queries_two = split_heads(query_two, local_heads)
@@ -179,15 +231,15 @@
         queries_two, keys_mem, values_mem, cross_allowed, 0.0, factor
     )
     attend_two = merge_heads(attended_two).astype(low_type)
-    stream_two = stream_one + head_sum(matmul("tw,wd->td", attend_two, out_cross))
+    stream_two = stream_one + head_sum(matmul("tw,dw->td", attend_two, out_cross))
     normed_three = norm_apply(stream_two, gain_ff.astype(jnp.float32)).astype(low_type)
     hidden_pre = matmul("td,df->tf", normed_three, ff_up)
     active = jax.nn.gelu(hidden_pre).astype(low_type)
-    stream_out = stream_two + head_sum(matmul("tf,fd->td", active, ff_down))
+    stream_out = stream_two + head_sum(matmul("tf,df->td", active, ff_down))
     mixed = stream_out.astype(low_type)
     grad_out = out_grad.astype(jnp.float32)
-    grad_down = matmul("tf,td->fd", active, out_grad)
-    grad_active = matmul("td,fd->tf", out_grad, ff_down)
+    grad_down = matmul("td,tf->df", out_grad, active)
+    grad_active = matmul("td,df->tf", out_grad, ff_down)
     gelu_value, gelu_pull = jax.vjp(jax.nn.gelu, hidden_pre)
     grad_pre = gelu_pull(grad_active)[0].astype(low_type)
     grad_up = matmul("td,tf->df", normed_three, grad_pre)
@@ -195,15 +247,11 @@
     norm_value, norm_pull = jax.vjp(norm_apply, stream_two, gain_ff.astype(jnp.float32))
     grad_stream_three, grad_gain_ff = norm_pull(grad_normed_three)
     grad_two = grad_out + grad_stream_three
-    ff_summed = (
-        lax.psum_scatter(grad_gain_ff, "seq", scatter_dimension=0, tiled=True),
-        lax.psum_scatter(grad_up, "seq", scatter_dimension=0, tiled=True),
-        lax.psum_scatter(grad_down, "seq", scatter_dimension=1, tiled=True),
-    )
+    ff_summed = scatter_rows(jnp.concatenate([grad_up, grad_down], axis=1), "seq")
     low_two = grad_two.astype(low_type)
-    grad_out_cross = matmul("tw,td->wd", attend_two, low_two)
+    grad_out_cross = matmul("td,tw->dw", low_two, attend_two)
     grad_attend_two = split_heads(
-        matmul("td,wd->tw", low_two, out_cross).astype(low_type), local_heads
+        matmul("td,dw->tw", low_two, out_cross).astype(low_type), local_heads
     )
     grad_queries_two, grad_mem_keys, grad_mem_values, unused_scores = attend_backward(
         queries_two, keys_mem, values_mem, cross_allowed, 0.0, logsum_two, grad_attend_two, factor
@@ -214,15 +262,11 @@
     norm_value, norm_pull = jax.vjp(norm_apply, stream_one, gain_cross.astype(jnp.float32))
     grad_stream_two, grad_gain_cross = norm_pull(grad_normed_two)
     grad_one = grad_two + grad_stream_two
-    cross_summed = (
-        lax.psum_scatter(grad_gain_cross, "seq", scatter_dimension=0, tiled=True),
-        lax.psum_scatter(grad_query_cross, "seq", scatter_dimension=0, tiled=True),
-        lax.psum_scatter(grad_out_cross, "seq", scatter_dimension=1, tiled=True),
-    )
+    cross_summed = scatter_rows(jnp.concatenate([grad_query_cross, grad_out_cross], axis=1), "seq")
     low_one = grad_one.astype(low_type)
-    grad_out_self = matmul("tw,td->wd", attend_one, low_one)
+    grad_out_self = matmul("td,tw->dw", low_one, attend_one)
     grad_attend_one = split_heads(
-        matmul("td,wd->tw", low_one, out_self).astype(low_type), local_heads
+        matmul("td,dw->tw", low_one, out_self).astype(low_type), local_heads
     )
     grad_queries_one, grad_keys_self, grad_values_self, grad_scores = attend_backward(
         queries_one,
@@ -267,48 +311,33 @@
     norm_value, norm_pull = jax.vjp(norm_apply, stream_in, gain_self.astype(jnp.float32))
     grad_stream_one, grad_gain_self = norm_pull(grad_normed_one)
     grad_hidden = grad_one + grad_stream_one
-    rest_summed = (
-        lax.psum_scatter(grad_gain_self, "seq", scatter_dimension=0, tiled=True),
-        lax.psum_scatter(grad_query_self, "seq", scatter_dimension=0, tiled=True),
-        lax.psum_scatter(grad_key_self, "seq", scatter_dimension=0, tiled=True),
-        lax.psum_scatter(grad_value_self, "seq", scatter_dimension=0, tiled=True),
-        lax.psum_scatter(grad_out_self, "seq", scatter_dimension=1, tiled=True),
-        lax.psum_scatter(grad_key_cross, "seq", scatter_dimension=0, tiled=True),
-        lax.psum_scatter(grad_value_cross, "seq", scatter_dimension=0, tiled=True),
-    )
-    summed = (
-        rest_summed[0],
-        rest_summed[1],
-        rest_summed[2],
-        rest_summed[3],
-        rest_summed[4],
-        cross_summed[0],
-        cross_summed[1],
-        rest_summed[5],
-        rest_summed[6],
-        cross_summed[2],
-        ff_summed[0],
-        ff_summed[1],
-        ff_summed[2],
-    )
-    grad_table = lax.psum(grad_table_part, "seq")
+    gain_grads = jnp.pad(jnp.stack([grad_gain_self, grad_gain_cross, grad_gain_ff], axis=1), ((0, 0), (0, 125)))
+    rest_summed = scatter_rows(
+        jnp.concatenate(
+            [gain_grads, grad_query_self, grad_key_self, grad_value_self, grad_out_self, grad_key_cross, grad_value_cross],
+            axis=1,
+        ),
+        "seq",
+    )
+    rest = [rest_summed[:, 128 + i * part : 128 + (i + 1) * part] for i in range(6)]
+    grad_table = sum_all(grad_table_part, "seq")
     return (
         mixed,
         grad_hidden,
         grad_memory,
-        summed[0],
-        summed[1],
-        summed[2],
-        summed[3],
-        summed[4],
-        summed[5],
-        summed[6],
-        summed[7],
-        summed[8],
-        summed[9],
-        summed[10],
-        summed[11],
-        summed[12],
+        rest_summed[:, 0],
+        rest[0],
+        rest[1],
+        rest[2],
+        rest[3].T,
+        rest_summed[:, 1],
+        cross_summed[:, :part],
+        rest[4],
+        rest[5],
+        cross_summed[:, part:].T,
+        rest_summed[:, 2],
+        ff_summed[:, :wide],
+        ff_summed[:, wide:].T,
         grad_table,
     )
 

time: 2090 us -> 509 us (0.24)
  waiting for transfers between devices: 1350 us -> 153 us
  blocking collectives: 447 us -> 0 us
  starting transfers between devices: 17.8 us -> 93.8 us
  matrix products: 165 us -> 135 us
    reduce_scatter x8 -> x0, waiting for transfers between devices: 930 us -> none  [the longest x1 143 us: per_device(): lax.psum_scatter(grad_down, 'seq', scatter_dimension=1, tiled=True)]
    all_gather x8 -> x0, blocking collectives: 341 us -> none  [the longest x1 44.4 us: per_device(): lax.all_gather(self_v.astype(low_type), 'seq', axis=0, tiled=True)]
    unnamed x19 -> x0, waiting for transfers between devices: 258 us -> none
    ppermute x0 -> x59, waiting for transfers between devices: none -> 130 us  [the longest x52 130 us: partner_swap(): return lax.ppermute(value, axis, [(i, i ^ 1 << bit) for i in range(count)])]
    unnamed x2 -> x0, blocking collectives: 106 us -> none
    all_gather x2 -> x0, waiting for transfers between devices: 101 us -> none  [the longest x1 59.1 us: per_device(): lax.all_gather(ff_in.astype(low_type), 'seq', axis=0, tiled=True)]
    ppermute x0 -> x59, starting transfers between devices: none -> 64.9 us  [the longest x52 64 us: partner_swap(): return lax.ppermute(value, axis, [(i, i ^ 1 << bit) for i in range(count)])]
    psum x5 -> x0, waiting for transfers between devices: 34.5 us -> none  [head_sum(): return lax.psum(values, 'heads')]
  transfers between devices with their start and end apart: 25 -> 67, of which waited for: 19 -> 29; matrix products, arithmetic and copies ran while one was open for 6% -> 45% of each run, Pallas kernels for 0% -> 0%
where the time goes in v1:
time: 509 us; the launch traced here: 503 us
  waiting for transfers between devices  153 us (30%)
  matrix products  135 us (27%)
  starting transfers between devices  93.8 us (18%)
  other arithmetic  73 us (14%)
  local copies, waits for them, and re-layouts  45 us (9%)
    ppermute x52, waiting for transfers between devices, partner_swap(): return lax.ppermute(value, axis, [(i, i ^ 1 << bit) for i in range(count)])  130 us
    dot_general x43, matrix products, matmul(): return jnp.einsum(spec, left, right, preferred_element_type=jnp.float32)  109 us
    ppermute x52, starting transfers between devices, partner_swap(): return lax.ppermute(value, axis, [(i, i ^ 1 << bit) for i in range(count)])  64 us
    ppermute x8, starting transfers between devices, shifted(): lax.ppermute(value, axis, [(source, source + steps) for source in range(l...  29 us
    dot_general x1, matrix products, per_device(): jnp.einsum('ijb,bh->hij', pair_table.astype(jnp.float32), bias_table, pre...  25.8 us
    ppermute x8, waiting for transfers between devices, shifted(): lax.ppermute(value, axis, [(source, source + steps) for source in range(l...  23.6 us
    convert_element_type x2, other arithmetic, attend_backward(): grad_scores = (weights * (grad_weights - inner)).astype(jnp.bfloat16)  12.6 us
    another operation x48, other arithmetic, gather_rows(): jnp.stack([jnp.where(mine, value, other), jnp.where(mine, other, value)],...  12.4 us
  transfers between devices with their start and end apart: 67, of which 29 were waited for; matrix products, arithmetic and copies ran while one was open for 45% of the time, Pallas kernels for 0%

profile of v1, /device:TPU:2, one launch (start us, length us, event | category | flops | bytes accessed | tf_op | source)
XLA Modules:
  0.0 502.9 jit_solution(18068259592559357299)
XLA Ops:
  21.5 25.8 %fusion.1 = f32[512,1024,6]{1,2,0:T(8,128)} fusion(s32[512,1024]{1,0:T(8,128)S(1)} %iota_subtract_fusion, s32[32]{0:T(128)S(1)} %get-tuple-element.101, s32[32]{0:T(128)S(1)} %get-tuple-element.100, f32[32,6]{0,1:T(8,128)S(1)} %copy-done.92), kind=kOutput, calls=%fused_computation.2 | convolution fusion | flops 1258291200 | bytes 14681088 | tf_op jit(solution)/shard_map/ijb,bh->hij/dot_general | solution.py:206
  63.8 3.7 collective-permute-done.15
  85.0 6.8 %collective-permute-done.3 = bf16[2,2,2,48,640]{4,3,2,1,0:T(8,128)(2,1)S(1)} collective-permute-done((bf16[2,2,2,48,640]{4,3,2,1,0:T(8,128)(2,1)S(1)}, bf16[2,2,2,48,640]{4,3,2,1,0:T(8,128)(2,1)S(1)}, u32[]{:S(2)}, u32[]{:S(2)}) %collective-permute-start.3) | collective-permute-done | bytes 491552 | tf_op jit(solution)/shard_map/ppermute | solution.py:78
  100.7 3.7 collective-permute-done.28
  108.6 10.5 %collective-permute-done.13 = bf16[2,2,2,48,896]{4,3,2,1,0:T(8,128)(2,1)S(1)} collective-permute-done((bf16[2,2,2,48,896]{4,3,2,1,0:T(8,128)(2,1)S(1)}, bf16[2,2,2,48,896]{4,3,2,1,0:T(8,128)(2,1)S(1)}, u32[]{:S(2)}, u32[]{:S(2)}) %collective-permute-start.13) | collective-permute-done | bytes 688160 | tf_op jit(solution)/shard_map/ppermute | solution.py:78
  120.1 7.5 %collective-permute-done.8 = bf16[512,384]{1,0:T(8,128)(2,1)S(1)} collective-permute-done((bf16[512,384]{1,0:T(8,128)(2,1)S(1)}, bf16[512,384]{1,0:T(8,128)(2,1)S(1)}, u32[]{:S(2)}, u32[]{:S(2)}) %collective-permute-start.8) | collective-permute-done | bytes 393248 | tf_op jit(solution)/shard_map/ppermute | solution.py:13
  137.2 15.2 %fusion.130 = (f32[6,512]{1,0:T(8,128)S(1)}, f32[6,512,1024]{2,1,0:T(8,128)S(1)}) fusion(f32[512,1024,6]{1,2,0:T(8,128)} %fusion.1, bf16[512,6,64]{0,2,1:T(8,128)(2,1)} %bitcast.430, bf16[1024,6,64]{0,2,1:T(8,128)(2,1)} %bitcast.401, pred[512,1024]{1,0:T(8,128)(4,1)S(1)} %get-tuple-element.99), kind=kOutput, calls=%fused_computation.352 | convolution fusion | flops 415233024 | bytes 26882048 | tf_op jit(solution)/shard_map/ihd,jhd->hij/dot_general | solution.py:25
  169.3 3.4 collective-permute-start.20
  173.5 5.8 %collective-permute-done.19 = bf16[512,384]{0,1:T(8,128)(2,1)S(1)} collective-permute-done((bf16[512,384]{0,1:T(8,128)(2,1)S(1)}, bf16[512,384]{0,1:T(8,128)(2,1)S(1)}, u32[]{:S(2)}, u32[]{:S(2)}) %collective-permute-start.19) | collective-permute-done | bytes 393248 | tf_op jit(solution)/shard_map/ppermute | solution.py:13
  179.3 8.3 %collective-permute-done.20 = bf16[512,384]{0,1:T(8,128)(2,1)S(1)} collective-permute-done((bf16[512,384]{0,1:T(8,128)(2,1)S(1)}, bf16[512,384]{0,1:T(8,128)(2,1)S(1)}, u32[]{:S(2)}, u32[]{:S(2)}) %collective-permute-start.20) | collective-permute-done | bytes 393248 | tf_op jit(solution)/shard_map/ppermute | solution.py:13
  200.9 11.6 %collective-permute-done.25 = bf16[2,2,2,48,1536]{4,3,2,1,0:T(8,128)(2,1)S(1)} collective-permute-done((bf16[2,2,2,48,1536]{4,3,2,1,0:T(8,128)(2,1)S(1)}, bf16[2,2,2,48,1536]{4,3,2,1,0:T(8,128)(2,1)S(1)}, u32[]{:S(2)}, u32[]{:S(2)}) %collective-permute-start.25) | collective-permute-done | bytes 1179680 | tf_op jit(solution)/shard_map/ppermute | solution.py:78
  227.5 21.7 %collective-permute-done.59 = bf16[2,2,2,48,1536]{4,3,0,1,2:T(8,128)(2,1)S(1)} collective-permute-done((bf16[2,2,2,48,1536]{4,3,0,1,2:T(8,128)(2,1)S(1)}, bf16[2,2,2,48,1536]{4,3,0,1,2:T(8,128)(2,1)S(1)}, u32[]{:S(2)}, u32[]{:S(2)}) %collective-permute-start.59) | collective-permute-done | bytes 1179680 | tf_op jit(solution)/shard_map/ppermute | solution.py:78
  262.8 6.3 %multiply_reduce_fusion.1 = (f32[6,512]{1,0:T(8,128)S(1)}, f32[6,512,1024]{2,1,0:T(8,128)}) fusion(f32[6,512,1024]{2,1,0:T(8,128)S(1)} %get-tuple-element.105, f32[6,512]{1,0:T(8,128)S(1)} %log_add_fusion.1, bf16[512,6,64]{0,2,1:T(8,128)(2,1)S(1)} %bitcast.415, bf16[1024,6,64]{0,2,1:T(8,128)(2,1)S(1)} %bitcast.421), kind=kOutput, calls=%fused_computation.15 | convolution fusion | flops 412087296 | bytes 26370048 | tf_op jit(solution)/shard_map/ihd,jhd->hij/dot_general | solution.py:25
  269.1 6.2 %multiply_convert_fusion.1 = bf16[6,512,1024]{2,1,0:T(8,128)(2,1)S(1)} fusion(f32[6,512,1024]{2,1,0:T(8,128)} %get-tuple-element.107, f32[6,512,1024]{2,1,0:T(8,128)S(1)} %get-tuple-element.105, f32[6,512]{1,0:T(8,128)S(1)} %get-tuple-element.106, f32[6,512]{1,0:T(8,128)S(1)} %log_add_fusion.1), kind=kLoop, calls=%fused_computation.14 | loop fusion | flops 12582912 | bytes 31481856 | tf_op jit(solution)/shard_map/convert_element_type | solution.py:59
  289.9 4.8 fusion.44
  298.1 5.8 %collective-permute-start.61 = (bf16[2,48,1536]{2,1,0:T(8,128)(2,1)S(1)}, bf16[2,48,1536]{2,1,0:T(8,128)(2,1)S(1)}, u32[]{:S(2)}, u32[]{:S(2)}) collective-permute-start(bf16[2,48,1536]{2,1,0:T(8,128)(2,1)S(1)} %fusion.88), channel_id=1, source_target_pairs={{0,8},{2,10},{4,12},{6,14},{8,0},{10,2},{12,4},{14,6},{16,24},{18,... | collective-permute-start | bytes 884744 | tf_op jit(solution)/shard_map/ppermute | solution.py:78
  308.4 6.0 %collective-permute-start.57 = (bf16[2,48,1536]{2,1,0:T(8,128)(2,1)S(1)}, bf16[2,48,1536]{2,1,0:T(8,128)(2,1)S(1)}, u32[]{:S(2)}, u32[]{:S(2)}) collective-permute-start(bf16[2,48,1536]{2,1,0:T(8,128)(2,1)S(1)} %fusion.87), channel_id=1, source_target_pairs={{0,8},{2,10},{4,12},{6,14},{8,0},{10,2},{12,4},{14,6},{16,24},{18,... | collective-permute-start | bytes 884744 | tf_op jit(solution)/shard_map/ppermute | solution.py:78
  321.1 3.4 collective-permute-start.62
  325.6 3.4 collective-permute-start.54
  329.2 7.8 %collective-permute-done.54 = bf16[48,384]{1,0:T(8,128)(2,1)S(1)} collective-permute-done((bf16[48,384]{1,0:T(8,128)(2,1)S(1)}, bf16[48,384]{1,0:T(8,128)(2,1)S(1)}, u32[]{:S(2)}, u32[]{:S(2)}) %collective-permute-start.54) | collective-permute-done | bytes 36896 | tf_op jit(solution)/shard_map/ppermute | solution.py:78
  346.6 3.4 fusion.41
  350.0 6.2 %multiply_reduce_fusion = (f32[6,512]{1,0:T(8,128)S(1)}, f32[6,512,1024]{2,1,0:T(8,128)}) fusion(f32[6,512,1024]{2,1,0:T(8,128)S(1)} %bitcast.380, f32[6,512]{1,0:T(8,128)S(1)} %log_add_fusion, bf16[512,6,64]{0,2,1:T(8,128)(2,1)S(1)} %bitcast.417, bf16[1024,6,64]{0,2,1:T(8,128)(2,1)S(1)} %bitcast.419), kind=kOutput, calls=%fused_computation.12 | convolution fusion | flops 412087296 | bytes 26370048 | tf_op jit(solution)/shard_map/ihd,jhd->hij/dot_general | solution.py:25
  356.3 6.4 %multiply_convert_fusion = bf16[6,512,1024]{2,1,0:T(8,128)(2,1)S(1)} fusion(f32[6,512,1024]{2,1,0:T(8,128)} %get-tuple-element.109, f32[6,512,1024]{2,1,0:T(8,128)S(1)} %bitcast.380, f32[6,512]{1,0:T(8,128)S(1)} %get-tuple-element.108, f32[6,512]{1,0:T(8,128)S(1)} %log_add_fusion), kind=kLoop, calls=%fused_computation.11 | loop fusion | flops 12582912 | bytes 31481856 | tf_op jit(solution)/shard_map/convert_element_type | solution.py:59
  362.7 19.4 %fusion.52 = f32[32,6]{0,1:T(8,128)S(1)} fusion(bf16[6,512,1024]{2,1,0:T(8,128)(2,1)S(1)} %multiply_convert_fusion, s32[512,1024]{1,0:T(8,128)S(1)} %copy-done.64, s32[32]{0:T(128)S(1)} %copy-done.91, s32[32]{0:T(128)S(1)} %copy-done.89), kind=kOutput, calls=%fused_computation.128 | convolution fusion | flops 251658240 | bytes 8389632 | tf_op jit(solution)/shard_map/hij,ijb->bh/dot_general | solution.py:25
  404.2 8.9 %collective-permute-start.33 = (bf16[512,384]{0,1:T(8,128)(2,1)}, bf16[512,384]{0,1:T(8,128)(2,1)S(1)}, u32[]{:S(2)}, u32[]{:S(2)}) collective-permute-start(bf16[512,384]{0,1:T(8,128)(2,1)} %bitcast.92), channel_id=1, source_target_pairs={{2,0},{4,2},{6,4},{8,6},{10,8},{12,10},{14,12},{16,14},{18,16},{20... | collective-permute-start | bytes 1179656 | tf_op jit(solution)/shard_map/ppermute | solution.py:13
  418.2 5.5 %copy.103 = f32[768,1280]{1,0:T(8,128)} copy(f32[768,1280]{0,1:T(8,128)} %pad_maximum_fusion) | data formatting | bytes 7864320 | tf_op jit(solution)/shard_map/slice | solution.py:108
  439.0 8.5 %collective-permute-done.43 = bf16[2,2,2,48,1280]{4,3,2,1,0:T(8,128)(2,1)S(1)} collective-permute-done((bf16[2,2,2,48,1280]{4,3,2,1,0:T(8,128)(2,1)S(1)}, bf16[2,2,2,48,1280]{4,3,2,1,0:T(8,128)(2,1)S(1)}, u32[]{:S(2)}, u32[]{:S(2)}) %collective-permute-start.43) | collective-permute-done | bytes 983072 | tf_op jit(solution)/shard_map/ppermute | solution.py:78
  452.9 5.2 %copy.102 = f32[768,1152]{1,0:T(8,128)} copy(f32[768,1152]{0,1:T(8,128)} %pad_maximum_fusion.3) | data formatting | bytes 7077888 | tf_op jit(solution)/shard_map/slice | solution.py:108
  464.2 14.5 %collective-permute-done.39 = bf16[2,2,2,48,1152]{4,3,2,1,0:T(8,128)(2,1)S(1)} collective-permute-done((bf16[2,2,2,48,1152]{4,3,2,1,0:T(8,128)(2,1)S(1)}, bf16[2,2,2,48,1152]{4,3,2,1,0:T(8,128)(2,1)S(1)}, u32[]{:S(2)}, u32[]{:S(2)}) %collective-permute-start.39) | collective-permute-done | bytes 884768 | tf_op jit(solution)/shard_map/ppermute | solution.py:78
  480.4 7.2 %collective-permute-done.40 = bf16[2,2,48,1152]{3,2,1,0:T(8,128)(2,1)S(1)} collective-permute-done((bf16[2,2,48,1152]{3,2,1,0:T(8,128)(2,1)S(1)}, bf16[2,2,48,1152]{3,2,1,0:T(8,128)(2,1)S(1)}, u32[]{:S(2)}, u32[]{:S(2)}) %collective-permute-start.40) | collective-permute-done | bytes 442400 | tf_op jit(solution)/shard_map/ppermute | solution.py:78
  487.9 6.2 %collective-permute-done.41 = bf16[2,48,1152]{2,1,0:T(8,128)(2,1)S(1)} collective-permute-done((bf16[2,48,1152]{2,1,0:T(8,128)(2,1)S(1)}, bf16[2,48,1152]{2,1,0:T(8,128)(2,1)S(1)}, u32[]{:S(2)}, u32[]{:S(2)}) %collective-permute-start.41) | collective-permute-done | bytes 221216 | tf_op jit(solution)/shard_map/ppermute | solution.py:78
  497.2 3.9 collective-permute-done.42
  (524 shorter events, 236.7 us)
Async XLA Ops:
  5.0 42.5 %collective-permute-start = (bf16[48,640]{1,0:T(8,128)(2,1)S(1)}, bf16[48,640]{1,0:T(8,128)(2,1)}, u32[]{:S(2)}, u32[]{:S(2)}) collective-permute-start(bf16[48,640]{1,0:T(8,128)(2,1)S(1)} %get-tuple-element.92), channel_id=1, source_target_pairs={{0,16},{2,18},{4,20},{6,22},{8,24},{10,26},{12,28},{14,30},{16,0},... | collective-permute-start | bytes 184328 | tf_op jit(solution)/shard_map/ppermute | solution.py:78
  7.6 41.1 %collective-permute-start.4 = (bf16[48,640]{1,0:T(8,128)(2,1)S(1)}, bf16[48,640]{1,0:T(8,128)(2,1)}, u32[]{:S(2)}, u32[]{:S(2)}) collective-permute-start(bf16[48,640]{1,0:T(8,128)(2,1)S(1)} %get-tuple-element.93), channel_id=1, source_target_pairs={{0,16},{2,18},{4,20},{6,22},{8,24},{10,26},{12,28},{14,30},{16,0},... | collective-permute-start | bytes 184328 | tf_op jit(solution)/shard_map/ppermute | solution.py:78
  10.7 40.6 %collective-permute-start.10 = (bf16[48,896]{1,0:T(8,128)(2,1)S(1)}, bf16[48,896]{1,0:T(8,128)(2,1)}, u32[]{:S(2)}, u32[]{:S(2)}) collective-permute-start(bf16[48,896]{1,0:T(8,128)(2,1)S(1)} %pad_maximum_fusion.38), channel_id=1, source_target_pairs={{0,16},{2,18},{4,20},{6,22},{8,24},{10,26},{12,28},{14,30},{16,0},... | collective-permute-start | bytes 258056 | tf_op jit(solution)/shard_map/ppermute | solution.py:78
  14.3 38.5 %collective-permute-start.14 = (bf16[48,1024]{1,0:T(8,128)(2,1)S(1)}, bf16[48,1024]{1,0:T(8,128)(2,1)S(1)}, u32[]{:S(2)}, u32[]{:S(2)}) collective-permute-start(bf16[48,1024]{1,0:T(8,128)(2,1)S(1)} %pad_maximum_fusion.36), channel_id=1, source_target_pairs={{0,16},{2,18},{4,20},{6,22},{8,24},{10,26},{12,28},{14,30},{16,0},... | collective-permute-start | bytes 294920 | tf_op jit(solution)/shard_map/ppermute | solution.py:78
  14.7 39.7 %collective-permute-start.26 = (bf16[48,1536]{1,0:T(8,128)(2,1)S(1)}, bf16[48,1536]{1,0:T(8,128)(2,1)S(1)}, u32[]{:S(2)}, u32[]{:S(2)}) collective-permute-start(bf16[48,1536]{1,0:T(8,128)(2,1)S(1)} %convert_bitcast_fusion.1), channel_id=1, source_target_pairs={{0,16},{2,18},{4,20},{6,22},{8,24},{10,26},{12,28},{14,30},{16,0},... | collective-permute-start | bytes 442376 | tf_op jit(solution)/shard_map/ppermute | solution.py:78
  57.0 21.4 %collective-permute-start.23 = (bf16[2,48,1536]{2,1,0:T(8,128)(2,1)S(1)}, bf16[2,48,1536]{2,1,0:T(8,128)(2,1)S(1)}, u32[]{:S(2)}, u32[]{:S(2)}) collective-permute-start(bf16[2,48,1536]{2,1,0:T(8,128)(2,1)S(1)} %pad_maximum_fusion.28), channel_id=1, source_target_pairs={{0,8},{2,10},{4,12},{6,14},{8,0},{10,2},{12,4},{14,6},{16,24},{18,... | collective-permute-start | bytes 884744 | tf_op jit(solution)/shard_map/ppermute | solution.py:78
  70.8 21.0 %collective-permute-start.3 = (bf16[2,2,2,48,640]{4,3,2,1,0:T(8,128)(2,1)S(1)}, bf16[2,2,2,48,640]{4,3,2,1,0:T(8,128)(2,1)S(1)}, u32[]{:S(2)}, u32[]{:S(2)}) collective-permute-start(bf16[2,2,2,48,640]{4,3,2,1,0:T(8,128)(2,1)S(1)} %pad_maximum_fusion.24), channel_id=1, source_target_pairs={{0,2},{2,0},{4,6},{6,4},{8,10},{10,8},{12,14},{14,12},{16,18},{18,... | collective-permute-start | bytes 1474568 | tf_op jit(solution)/shard_map/ppermute | solution.py:78
  78.4 26.0 %collective-permute-start.28 = (bf16[2,2,48,1536]{3,2,0,1:T(8,128)(2,1)S(1)}, bf16[2,2,48,1536]{3,2,0,1:T(8,128)(2,1)S(1)}, u32[]{:S(2)}, u32[]{:S(2)}) collective-permute-start(bf16[2,2,48,1536]{3,2,0,1:T(8,128)(2,1)S(1)} %pad_maximum_fusion.23), channel_id=1, source_target_pairs={{0,2},{2,0},{4,6},{6,4},{8,10},{10,8},{12,14},{14,12},{16,18},{18,... | collective-permute-start | bytes 1769480 | tf_op jit(solution)/shard_map/ppermute | solution.py:78
  80.0 83.7 %collective-permute-start.24 = (bf16[2,2,48,1536]{3,2,1,0:T(8,128)(2,1)}, bf16[2,2,48,1536]{3,2,1,0:T(8,128)(2,1)}, u32[]{:S(2)}, u32[]{:S(2)}) collective-permute-start(bf16[2,2,48,1536]{3,2,1,0:T(8,128)(2,1)} %pad_maximum_fusion.22), channel_id=1, source_target_pairs={{0,4},{2,6},{4,0},{6,2},{8,12},{10,14},{12,8},{14,10},{16,20},{18,... | collective-permute-start | bytes 1769480 | tf_op jit(solution)/shard_map/ppermute | solution.py:78
  81.6 37.6 %collective-permute-start.13 = (bf16[2,2,2,48,896]{4,3,2,1,0:T(8,128)(2,1)S(1)}, bf16[2,2,2,48,896]{4,3,2,1,0:T(8,128)(2,1)S(1)}, u32[]{:S(2)}, u32[]{:S(2)}) collective-permute-start(bf16[2,2,2,48,896]{4,3,2,1,0:T(8,128)(2,1)S(1)} %pad_maximum_fusion.19), channel_id=1, source_target_pairs={{0,2},{2,0},{4,6},{6,4},{8,10},{10,8},{12,14},{14,12},{16,18},{18,... | collective-permute-start | bytes 2064392 | tf_op jit(solution)/shard_map/ppermute | solution.py:78
  91.8 68.5 %collective-permute-start.17 = (bf16[2,2,2,48,1024]{4,3,0,1,2:T(8,128)(2,1)}, bf16[2,2,2,48,1024]{4,3,0,1,2:T(8,128)(2,1)}, u32[]{:S(2)}, u32[]{:S(2)}) collective-permute-start(bf16[2,2,2,48,1024]{4,3,0,1,2:T(8,128)(2,1)} %pad_maximum_fusion.16), channel_id=1, source_target_pairs={{0,4},{2,6},{4,0},{6,2},{8,12},{10,14},{12,8},{14,10},{16,20},{18,... | collective-permute-start | bytes 2359304 | tf_op jit(solution)/shard_map/ppermute | solution.py:78
  94.8 32.8 %collective-permute-start.8 = (bf16[512,384]{1,0:T(8,128)(2,1)S(1)}, bf16[512,384]{1,0:T(8,128)(2,1)S(1)}, u32[]{:S(2)}, u32[]{:S(2)}) collective-permute-start(bf16[512,384]{1,0:T(8,128)(2,1)S(1)} %convolution_convert_fusion.7), channel_id=1, source_target_pairs={{0,2},{2,4},{4,6},{6,8},{8,10},{10,12},{12,14},{14,16},{16,18},{18... | collective-permute-start | bytes 1179656 | tf_op jit(solution)/shard_map/ppermute | solution.py:13
  104.4 28.4 %collective-permute-start.9 = (bf16[512,384]{1,0:T(8,128)(2,1)}, bf16[512,384]{1,0:T(8,128)(2,1)}, u32[]{:S(2)}, u32[]{:S(2)}) collective-permute-start(bf16[512,384]{1,0:T(8,128)(2,1)} %convolution_convert_fusion.5), channel_id=1, source_target_pairs={{0,2},{2,4},{4,6},{6,8},{8,10},{10,12},{12,14},{14,16},{16,18},{18... | collective-permute-start | bytes 1179656 | tf_op jit(solution)/shard_map/ppermute | solution.py:13
  119.2 79.4 %collective-permute-start.29 = (bf16[2,2,2,48,1536]{4,3,0,1,2:T(8,128)(2,1)}, bf16[2,2,2,48,1536]{4,3,0,1,2:T(8,128)(2,1)}, u32[]{:S(2)}, u32[]{:S(2)}) collective-permute-start(bf16[2,2,2,48,1536]{4,3,0,1,2:T(8,128)(2,1)} %pad_maximum_fusion.11), channel_id=1, source_target_pairs={{0,4},{2,6},{4,0},{6,2},{8,12},{10,14},{12,8},{14,10},{16,20},{18,... | collective-permute-start | bytes 3538952 | tf_op jit(solution)/shard_map/ppermute | solution.py:78
  163.6 24.1 %collective-permute-start.18 = (f32[512,768]{1,0:T(8,128)S(1)}, f32[512,768]{1,0:T(8,128)S(1)}, u32[]{:S(2)}, u32[]{:S(2)}) collective-permute-start(f32[512,768]{1,0:T(8,128)S(1)} %fusion.132), channel_id=1, source_target_pairs={{0,1},{1,0},{2,3},{3,2},{4,5},{5,4},{6,7},{7,6},{8,9},{9,8},{10,11... | collective-permute-start | bytes 4718600 | tf_op jit(solution)/shard_map/ppermute | solution.py:37
  172.9 39.6 %collective-permute-start.25 = (bf16[2,2,2,48,1536]{4,3,2,1,0:T(8,128)(2,1)S(1)}, bf16[2,2,2,48,1536]{4,3,2,1,0:T(8,128)(2,1)S(1)}, u32[]{:S(2)}, u32[]{:S(2)}) collective-permute-start(bf16[2,2,2,48,1536]{4,3,2,1,0:T(8,128)(2,1)S(1)} %pad_maximum_fusion.10), channel_id=1, source_target_pairs={{0,2},{2,0},{4,6},{6,4},{8,10},{10,8},{12,14},{14,12},{16,18},{18,... | collective-permute-start | bytes 3538952 | tf_op jit(solution)/shard_map/ppermute | solution.py:78
  221.6 27.6 %collective-permute-start.59 = (bf16[2,2,2,48,1536]{4,3,0,1,2:T(8,128)(2,1)S(1)}, bf16[2,2,2,48,1536]{4,3,0,1,2:T(8,128)(2,1)S(1)}, u32[]{:S(2)}, u32[]{:S(2)}) collective-permute-start(bf16[2,2,2,48,1536]{4,3,0,1,2:T(8,128)(2,1)S(1)} %fusion.51), channel_id=1, source_target_pairs={{0,4},{2,6},{4,0},{6,2},{8,12},{10,14},{12,8},{14,10},{16,20},{18,... | collective-permute-start | bytes 3538952 | tf_op jit(solution)/shard_map/ppermute | solution.py:78
  223.1 32.2 %collective-permute-start.31 = (f32[512,768]{1,0:T(8,128)S(1)}, f32[512,768]{1,0:T(8,128)S(1)}, u32[]{:S(2)}, u32[]{:S(2)}) collective-permute-start(f32[512,768]{1,0:T(8,128)S(1)} %fusion.133), channel_id=1, source_target_pairs={{0,1},{1,0},{2,3},{3,2},{4,5},{5,4},{6,7},{7,6},{8,9},{9,8},{10,11... | collective-permute-start | bytes 4718600 | tf_op jit(solution)/shard_map/ppermute | solution.py:37
  224.8 28.8 %collective-permute-start.55 = (bf16[2,2,2,48,1536]{4,3,0,1,2:T(8,128)(2,1)S(1)}, bf16[2,2,2,48,1536]{4,3,0,1,2:T(8,128)(2,1)S(1)}, u32[]{:S(2)}, u32[]{:S(2)}) collective-permute-start(bf16[2,2,2,48,1536]{4,3,0,1,2:T(8,128)(2,1)S(1)} %fusion.50), channel_id=1, source_target_pairs={{0,2},{2,0},{4,6},{6,4},{8,10},{10,8},{12,14},{14,12},{16,18},{18,... | collective-permute-start | bytes 3538952 | tf_op jit(solution)/shard_map/ppermute | solution.py:78
  226.9 29.1 %collective-permute-start.30 = (f32[512,768]{1,0:T(8,128)S(1)}, f32[512,768]{1,0:T(8,128)S(1)}, u32[]{:S(2)}, u32[]{:S(2)}) collective-permute-start(f32[512,768]{1,0:T(8,128)S(1)} %fusion.115), channel_id=1, source_target_pairs={{0,1},{1,0},{2,3},{3,2},{4,5},{5,4},{6,7},{7,6},{8,9},{9,8},{10,11... | collective-permute-start | bytes 4718600 | tf_op jit(solution)/shard_map/ppermute | solution.py:37
  252.2 44.4 %collective-permute-start.60 = (bf16[2,2,48,1536]{3,2,0,1:T(8,128)(2,1)}, bf16[2,2,48,1536]{3,2,0,1:T(8,128)(2,1)}, u32[]{:S(2)}, u32[]{:S(2)}) collective-permute-start(bf16[2,2,48,1536]{3,2,0,1:T(8,128)(2,1)} %fusion.62), channel_id=1, source_target_pairs={{0,2},{2,0},{4,6},{6,4},{8,10},{10,8},{12,14},{14,12},{16,18},{18,... | collective-permute-start | bytes 1769480 | tf_op jit(solution)/shard_map/ppermute | solution.py:78
  255.0 43.1 %collective-permute-start.56 = (bf16[2,2,48,1536]{3,2,0,1:T(8,128)(2,1)}, bf16[2,2,48,1536]{3,2,0,1:T(8,128)(2,1)}, u32[]{:S(2)}, u32[]{:S(2)}) collective-permute-start(bf16[2,2,48,1536]{3,2,0,1:T(8,128)(2,1)} %fusion.61), channel_id=1, source_target_pairs={{0,4},{2,6},{4,0},{6,2},{8,12},{10,14},{12,8},{14,10},{16,20},{18,... | collective-permute-start | bytes 1769480 | tf_op jit(solution)/shard_map/ppermute | solution.py:78
  283.3 25.1 %collective-permute-start.51 = (bf16[2,2,2,48,384]{4,3,2,1,0:T(8,128)(2,1)S(1)}, bf16[2,2,2,48,384]{4,3,2,1,0:T(8,128)(2,1)S(1)}, u32[]{:S(2)}, u32[]{:S(2)}) collective-permute-start(bf16[2,2,2,48,384]{4,3,2,1,0:T(8,128)(2,1)S(1)} %fusion.86), channel_id=1, source_target_pairs={{0,4},{2,6},{4,0},{6,2},{8,12},{10,14},{12,8},{14,10},{16,20},{18,... | collective-permute-start | bytes 884744 | tf_op jit(solution)/shard_map/ppermute | solution.py:78
  285.1 29.4 %collective-permute-start.37 = (bf16[512,384]{0,1:T(8,128)(2,1)S(1)}, bf16[512,384]{0,1:T(8,128)(2,1)S(1)}, u32[]{:S(2)}, u32[]{:S(2)}) collective-permute-start(bf16[512,384]{0,1:T(8,128)(2,1)S(1)} %bitcast.436), channel_id=1, source_target_pairs={{2,0},{4,2},{6,4},{8,6},{10,8},{12,10},{14,12},{16,14},{18,16},{20... | collective-permute-start | bytes 1179656 | tf_op jit(solution)/shard_map/ppermute | solution.py:13
  287.6 29.3 %collective-permute-start.36 = (bf16[512,384]{0,1:T(8,128)(2,1)S(1)}, bf16[512,384]{0,1:T(8,128)(2,1)S(1)}, u32[]{:S(2)}, u32[]{:S(2)}) collective-permute-start(bf16[512,384]{0,1:T(8,128)(2,1)S(1)} %bitcast.437), channel_id=1, source_target_pairs={{2,0},{4,2},{6,4},{8,6},{10,8},{12,10},{14,12},{16,14},{18,16},{20... | collective-permute-start | bytes 1179656 | tf_op jit(solution)/shard_map/ppermute | solution.py:13
  296.6 43.9 %collective-permute-start.32 = (f32[512,768]{1,0:T(8,128)S(1)}, f32[512,768]{1,0:T(8,128)S(1)}, u32[]{:S(2)}, u32[]{:S(2)}) collective-permute-start(f32[512,768]{1,0:T(8,128)S(1)} %fusion.68), channel_id=1, source_target_pairs={{0,1},{1,0},{2,3},{3,2},{4,5},{5,4},{6,7},{7,6},{8,9},{9,8},{10,11... | collective-permute-start | bytes 4718600 | tf_op jit(solution)/shard_map/ppermute | solution.py:37
  298.1 22.8 %collective-permute-start.61 = (bf16[2,48,1536]{2,1,0:T(8,128)(2,1)S(1)}, bf16[2,48,1536]{2,1,0:T(8,128)(2,1)S(1)}, u32[]{:S(2)}, u32[]{:S(2)}) collective-permute-start(bf16[2,48,1536]{2,1,0:T(8,128)(2,1)S(1)} %fusion.88), channel_id=1, source_target_pairs={{0,8},{2,10},{4,12},{6,14},{8,0},{10,2},{12,4},{14,6},{16,24},{18,... | collective-permute-start | bytes 884744 | tf_op jit(solution)/shard_map/ppermute | solution.py:78
  319.3 115.7 %collective-permute-start.38 = (f32[512,768]{1,0:T(8,128)}, f32[512,768]{1,0:T(8,128)}, u32[]{:S(2)}, u32[]{:S(2)}) collective-permute-start(f32[512,768]{1,0:T(8,128)} %convolution_add_fusion), channel_id=1, source_target_pairs={{0,1},{1,0},{2,3},{3,2},{4,5},{5,4},{6,7},{7,6},{8,9},{9,8},{10,11... | collective-permute-start | bytes 4718600 | tf_op jit(solution)/shard_map/ppermute | solution.py:37
  391.7 22.0 %collective-permute-start.47 = (bf16[2,2,2,48,384]{4,3,2,1,0:T(8,128)(2,1)S(1)}, bf16[2,2,2,48,384]{4,3,2,1,0:T(8,128)(2,1)S(1)}, u32[]{:S(2)}, u32[]{:S(2)}) collective-permute-start(bf16[2,2,2,48,384]{4,3,2,1,0:T(8,128)(2,1)S(1)} %fusion.85), channel_id=1, source_target_pairs={{0,2},{2,0},{4,6},{6,4},{8,10},{10,8},{12,14},{14,12},{16,18},{18,... | collective-permute-start | bytes 884744 | tf_op jit(solution)/shard_map/ppermute | solution.py:78
  393.5 20.4 %collective-permute-start.34 = (bf16[512,384]{0,1:T(8,128)(2,1)S(1)}, bf16[512,384]{0,1:T(8,128)(2,1)S(1)}, u32[]{:S(2)}, u32[]{:S(2)}) collective-permute-start(bf16[512,384]{0,1:T(8,128)(2,1)S(1)} %bitcast.438), channel_id=1, source_target_pairs={{2,0},{4,2},{6,4},{8,6},{10,8},{12,10},{14,12},{16,14},{18,16},{20... | collective-permute-start | bytes 1179656 | tf_op jit(solution)/shard_map/ppermute | solution.py:13
  404.2 23.1 %collective-permute-start.33 = (bf16[512,384]{0,1:T(8,128)(2,1)}, bf16[512,384]{0,1:T(8,128)(2,1)S(1)}, u32[]{:S(2)}, u32[]{:S(2)}) collective-permute-start(bf16[512,384]{0,1:T(8,128)(2,1)} %bitcast.92), channel_id=1, source_target_pairs={{2,0},{4,2},{6,4},{8,6},{10,8},{12,10},{14,12},{16,14},{18,16},{20... | collective-permute-start | bytes 1179656 | tf_op jit(solution)/shard_map/ppermute | solution.py:13
  425.5 22.0 %collective-permute-start.43 = (bf16[2,2,2,48,1280]{4,3,2,1,0:T(8,128)(2,1)S(1)}, bf16[2,2,2,48,1280]{4,3,2,1,0:T(8,128)(2,1)S(1)}, u32[]{:S(2)}, u32[]{:S(2)}) collective-permute-start(bf16[2,2,2,48,1280]{4,3,2,1,0:T(8,128)(2,1)S(1)} %fusion.55), channel_id=1, source_target_pairs={{0,4},{2,6},{4,0},{6,2},{8,12},{10,14},{12,8},{14,10},{16,20},{18,... | collective-permute-start | bytes 2949128 | tf_op jit(solution)/shard_map/ppermute | solution.py:78
  (133 other events, 1404.6 us)

commit v2 on v0

v2 whole, which is shorter than its diff:
```python
import functools

import jax
import jax.numpy as jnp
from jax import lax
from jax.experimental import pallas as pl
from jax.experimental.pallas import tpu as pltpu
from jax.sharding import Mesh, PartitionSpec as P

EPSILON = 1e-06
MASKED = -1000000000.0
LANES = 128
TILE = 256
VMEM_LIMIT = 56 * 2**20
GELU_ROOT = 0.7978845608028654
GELU_CUBE = 0.044715


def dot_nt(left, right):
    return lax.dot_general(left, right, (((1,), (1,)), ((), ())), preferred_element_type=jnp.float32)


def dot_nn(left, right):
    return jnp.dot(left, right, preferred_element_type=jnp.float32)


def dot_tn(left, right):
    return lax.dot_general(left, right, (((0,), (0,)), ((), ())), preferred_element_type=jnp.float32)


def low(value):
    return value.astype(jnp.bfloat16)


def full_block(shape):
    return pl.BlockSpec(shape, lambda i: (0,) * len(shape))


def params(flops, nbytes):
    return dict(
        compiler_params=pltpu.CompilerParams(vmem_limit_bytes=VMEM_LIMIT),
        cost_estimate=pl.CostEstimate(flops=flops, bytes_accessed=nbytes, transcendentals=0),
    )


def bias_kernel(rel_ref, table_ref, out_ref):
    heads, span = out_ref.shape[0], rel_ref.shape[1]
    count = span // LANES
    buckets = table_ref.shape[1]
    rel = rel_ref[...]
    by_distance = jnp.zeros((table_ref.shape[0], span), jnp.float32)
    for bucket in range(buckets):
        by_distance = jnp.where(rel == bucket, table_ref[:, bucket : bucket + 1], by_distance)
    rows = lax.broadcasted_iota(jnp.int32, (LANES, LANES), 0)
    cols = lax.broadcasted_iota(jnp.int32, (LANES, LANES), 1)
    for head in range(heads):
        line = by_distance[head : head + 1]
        for block in range(count):
            before = (block - 1) % count
            window = jnp.concatenate(
                [
                    line[:, block * LANES : (block + 1) * LANES],
                    line[:, before * LANES : (before + 1) * LANES],
                ],
                axis=1,
            )
            window = jnp.broadcast_to(window, (LANES, 2 * LANES))
            tile = pltpu.roll(window, 0, 1, stride=1, stride_axis=0)[:, :LANES]
            if block == 0:
                tile = jnp.where(cols >= rows, tile, MASKED)
            start = (count - 1 - block) * LANES
            out_ref[head, start : start + LANES, :] = tile
        out_ref[head, span : span + LANES, :] = jnp.full((LANES, LANES), MASKED, jnp.float32)


def bias_tiles(rel_row, bias_table):
    span = rel_row.shape[1]
    buckets, heads = bias_table.shape
    table = jnp.pad(bias_table.T, ((0, 8 - heads), (0, 0)))
    return pl.pallas_call(
        bias_kernel,
        out_shape=jax.ShapeDtypeStruct((heads, span + LANES, LANES), jnp.float32),
        name="bias_tiles",
        **params(10**9, 4 * 10**6),
    )(rel_row, table)


def head_lanes(values, head, size):
    lane = lax.broadcasted_iota(jnp.int32, values.shape, 1)
    return jnp.where((lane >= head * size) & (lane < (head + 1) * size), values, jnp.zeros_like(values))


def key_rows(causal, tile, rows, keys):
    return keys - rows + (tile + 1) * TILE if causal else keys


def bias_at(bias_ref, head, tile, rows, need):
    parts = []
    for sub in range(TILE // LANES):
        start = (rows // LANES - 1 - (tile * (TILE // LANES) + sub)) * LANES
        parts.append(bias_ref[head, start : start + need, :])
    return jnp.concatenate(parts, axis=1)


def attend(queries, k, v, seg_ref, own_ref, bias_ref, att_ref, p_ref, size):
    rows, keys = queries.shape[0], k.shape[0]
    causal = bias_ref is not None
    queries = queries * jnp.asarray(size**-0.5, queries.dtype)
    flipped = v.T
    for tile in range(rows // TILE):
        need = key_rows(causal, tile, rows, keys)
        span = slice(tile * TILE, (tile + 1) * TILE)
        allowed = own_ref[:, span] == seg_ref[:need, :]
        parts = []
        for head in range(LANES // size):
            scores = dot_nt(k[:need], head_lanes(queries[span], head, size))
            if causal:
                scores = scores + bias_at(bias_ref, head, tile, rows, need)
            scores = jnp.where(allowed, scores, MASKED)
            raised = jnp.exp(scores - jnp.max(scores, axis=0, keepdims=True))
            share = 1.0 / jnp.sum(raised, axis=0, keepdims=True)
            weights = low(raised * share)
            p_ref[head, :need, span] = weights
            parts.append(dot_nn(flipped[head * size : (head + 1) * size, :need], weights))
        att_ref[span, :] = low(jnp.concatenate(parts, axis=0).T)


def attend_back(queries, k, v, grads, p_ref, dq_ref, dk_ref, dv_ref, g_ref, size):
    rows, keys = queries.shape[0], k.shape[0]
    causal = g_ref is not None
    factor = size**-0.5
    flipped = k.T
    dk_sum = dv_sum = None
    for tile in reversed(range(rows // TILE)):
        need = key_rows(causal, tile, rows, keys)
        span = slice(tile * TILE, (tile + 1) * TILE)
        parts, all_ds, all_p, all_q, all_da = [], [], [], [], []
        for head in range(LANES // size):
            weights_low = p_ref[head, :need, span]
            weights = weights_low.astype(jnp.float32)
            grad_head = head_lanes(grads[span], head, size)
            grad_p = dot_nt(v[:need], grad_head)
            inner = jnp.sum(weights * grad_p, axis=0, keepdims=True)
            grad_s = low(weights * (grad_p - inner))
            parts.append(dot_nn(flipped[head * size : (head + 1) * size, :need], grad_s))
            all_ds.append(grad_s)
            all_p.append(weights_low)
            all_q.append(head_lanes(queries[span], head, size))
            all_da.append(grad_head)
            if causal:
                for sub in range(TILE // LANES):
                    start = (rows // LANES - 1 - (tile * (TILE // LANES) + sub)) * LANES
                    g_ref[head, start : start + need, :] += grad_s[
                        :, sub * LANES : (sub + 1) * LANES
                    ].astype(jnp.float32)
        dq_ref[span, :] = low((jnp.concatenate(parts, axis=0) * factor).T)
        dk = dot_nn(jnp.concatenate(all_ds, axis=1), jnp.concatenate(all_q, axis=0))
        dv = dot_nn(jnp.concatenate(all_p, axis=1), jnp.concatenate(all_da, axis=0))
        if dk_sum is None:
            dk_sum, dv_sum = dk, dv
        elif need < keys:
            dk_sum = jnp.concatenate([dk_sum[:need] + dk, dk_sum[need:]], axis=0)
            dv_sum = jnp.concatenate([dv_sum[:need] + dv, dv_sum[need:]], axis=0)
        else:
            dk_sum, dv_sum = dk_sum + dk, dv_sum + dv
    dk_ref[...] = low(dk_sum * factor)
    dv_ref[...] = low(dv_sum)


def left_roll(values, steps):
    return pltpu.roll(values, values.shape[1] - steps, 1) if steps else values


def by_bucket(g_ref, rel, table_ref, size):
    count = rel.shape[1] // LANES
    buckets = table_ref.shape[2]
    lane = lax.broadcasted_iota(jnp.int32, (1, buckets), 1)
    for head in range(LANES // size):
        line = None
        for group in range(LANES // 8):
            strip = jnp.concatenate(
                [
                    g_ref[head, (count - 1 - b) * LANES + group * 8 : (count - 1 - b) * LANES + group * 8 + 8, :]
                    for b in range(count)
                ],
                axis=1,
            )
            strip = left_roll(strip, group * 8)
            line = strip if line is None else line + strip
        row = lax.broadcasted_iota(jnp.int32, line.shape, 0)
        for bit in range(3):
            line = jnp.where((row >> bit) & 1 == 1, left_roll(line, 1 << bit), line)
        line = jnp.sum(line, axis=0, keepdims=True)
        found = jnp.zeros((1, buckets), jnp.float32)
        for bucket in range(buckets):
            total = jnp.sum(jnp.where(rel == bucket, line, 0.0), axis=1, keepdims=True)
            found = jnp.where(lane == bucket, total, found)
        table_ref[0, head : head + 1, :] = found


def norm_parts(values):
    scale = lax.rsqrt(jnp.mean(values * values, axis=-1, keepdims=True) + EPSILON)
    return values * scale, scale


def norm_backward(values, gain, grad):
    normed, scale = norm_parts(values)
    scaled = grad * gain
    mean = jnp.mean(scaled * normed, axis=-1, keepdims=True)
    return scale * (scaled - normed * mean), jnp.sum(grad * normed, axis=0, keepdims=True)


def group_lanes(step):
    return pl.ds(pl.multiple_of(step * LANES, LANES), LANES)


def self_project_kernel(prior_ref, own_ref, left_ref, right_ref, n_ref, q_ref, k_ref, v_ref, gain_ref):
    rows, part = q_ref.shape
    more = left_ref.shape[1] - part
    rest = part - more
    gains = right_ref[:, rest : rest + LANES].astype(jnp.float32).T[:8]
    gain_ref[...] = gains
    gain = gains[0:1]
    for at, source in ((0, prior_ref), (rows, own_ref)):
        span = slice(at, at + rows)
        n_ref[span, :] = low(norm_parts(source[...].astype(jnp.float32))[0] * gain)
    normed = n_ref[...]
    q_ref[...] = low(dot_nn(normed[rows:], left_ref[:, :part]))
    k_ref[:, :more] = low(dot_nn(normed, left_ref[:, part:]))
    k_ref[:, more:] = low(dot_nn(normed, right_ref[:, :rest]))
    v_ref[...] = low(dot_nn(normed, right_ref[:, rest + LANES :]))


def self_project(prior, own, left, right, part):
    rows, depth = own.shape
    shape = jax.ShapeDtypeStruct
    vmem = pl.BlockSpec(memory_space=pltpu.VMEM)
    return pl.pallas_call(
        self_project_kernel,
        in_specs=[vmem] * 4,
        out_specs=[vmem] * 5,
        out_shape=[
            shape((2 * rows, depth), jnp.bfloat16),
            shape((rows, part), jnp.bfloat16),
            shape((2 * rows, part), jnp.bfloat16),
            shape((2 * rows, part), jnp.bfloat16),
            shape((8, depth), jnp.float32),
        ],
        name="self_project",
        **params(4 * 10**9, 10 * 10**6),
    )(prior, own, left, right)


def self_forward_kernel(size, q_ref, k_ref, v_ref, seg_ref, row_ref, bias_ref, att_ref, p_ref):
    attend(q_ref[...], k_ref[...], v_ref[...], seg_ref, row_ref, bias_ref, att_ref, p_ref, size)


def self_forward(q, k, v, seg_col, own_row, bias, size):
    rows, part = q.shape
    keys = k.shape[0]
    heads = part // size
    pair = LANES // size
    shape = jax.ShapeDtypeStruct
    tall = lambda count: pl.BlockSpec((count, LANES), lambda i: (0, i))
    return pl.pallas_call(
        functools.partial(self_forward_kernel, size),
        grid=(part // LANES,),
        in_specs=[
            tall(rows),
            tall(keys),
            tall(keys),
            full_block(seg_col.shape),
            full_block(own_row.shape),
            pl.BlockSpec((pair,) + bias.shape[1:], lambda i: (i, 0, 0)),
        ],
        out_specs=[tall(rows), pl.BlockSpec((pair, keys, rows), lambda i: (i, 0, 0))],
        out_shape=[
            shape((rows, part), jnp.bfloat16),
            shape((heads, keys, rows), jnp.bfloat16),
        ],
        name="self_forward",
        **params(12 * 10**9, 20 * 10**6),
    )(q, k, v, seg_col, own_row, bias)


def cross_forward_kernel(
    size, at_q, at_o, x_ref, a_ref, b_ref, gain_ref, w_ref, k_ref, v_ref, seg_ref, row_ref,
    x1_ref, n_ref, q_ref, att_ref, p_ref, out_ref,
):
    step = pl.program_id(0)
    part = q_ref.shape[1]

    @pl.when(step == 0)
    def _():
        x1 = x_ref[...].astype(jnp.float32) + (a_ref[...] + b_ref[...])
        x1_ref[...] = x1
        normed = low(norm_parts(x1)[0] * gain_ref[1:2])
        n_ref[...] = normed
        q_ref[...] = low(dot_nn(normed, w_ref[:, at_q : at_q + part]))

    lanes = group_lanes(step)
    attend(q_ref[:, lanes], k_ref[...], v_ref[...], seg_ref, row_ref, None, att_ref.at[:, lanes], p_ref, size)

    @pl.when(step == pl.num_programs(0) - 1)
    def _():
        out_ref[...] = dot_nt(att_ref[...], w_ref[:, at_o : at_o + part])


def cross_forward(x, a, b, gains, weights, at_q, at_o, k, v, seg_col, own_row, size):
    rows, depth = x.shape
    keys, part = k.shape
    heads = part // size
    pair = LANES // size
    shape = jax.ShapeDtypeStruct
    return pl.pallas_call(
        functools.partial(cross_forward_kernel, size, at_q, at_o),
        grid=(part // LANES,),
        in_specs=[
            full_block(x.shape),
            full_block(a.shape),
            full_block(b.shape),
            full_block(gains.shape),
            full_block(weights.shape),
            pl.BlockSpec((keys, LANES), lambda i: (0, i)),
            pl.BlockSpec((keys, LANES), lambda i: (0, i)),
            full_block(seg_col.shape),
            full_block(own_row.shape),
        ],
        out_specs=[
            full_block((rows, depth)),
            full_block((rows, depth)),
            full_block((rows, part)),
            full_block((rows, part)),
            pl.BlockSpec((pair, keys, rows), lambda i: (i, 0, 0)),
            full_block((rows, depth)),
        ],
        out_shape=[
            shape((rows, depth), jnp.float32),
            shape((rows, depth), jnp.bfloat16),
            shape((rows, part), jnp.bfloat16),
            shape((rows, part), jnp.bfloat16),
            shape((heads, keys, rows), jnp.bfloat16),
            shape((rows, depth), jnp.float32),
        ],
        name="cross_forward",
        **params(12 * 10**9, 20 * 10**6),
    )(x, a, b, gains, weights, k, v, seg_col, own_row)


def feed_forward_kernel(
    x1_ref, a_ref, b_ref, gain_ref, g_ref, up_ref, down_ref,
    x2_ref, n_ref, act_ref, dpre_ref, mixed_ref, dn_ref,
):
    step = pl.program_id(0)

    @pl.when(step == 0)
    def _():
        x2 = x1_ref[...] + (a_ref[...] + b_ref[...])
        x2_ref[...] = x2
        n_ref[...] = low(norm_parts(x2)[0] * gain_ref[2:3])
        mixed_ref[...] = jnp.zeros_like(mixed_ref)
        dn_ref[...] = jnp.zeros_like(dn_ref)

    pre = dot_nn(n_ref[...], up_ref[...])
    square = pre * pre
    bend = jnp.tanh(GELU_ROOT * (pre + GELU_CUBE * (pre * square)))
    half = 0.5 * (1.0 + bend)
    act = low(pre * half)
    slope = half + (0.5 * GELU_ROOT) * pre * (1.0 - bend * bend) * (1.0 + (3 * GELU_CUBE) * square)
    grad_pre = low(slope * dot_nn(g_ref[...], down_ref[...]))
    act_ref[...] = act
    dpre_ref[...] = grad_pre
    mixed_ref[...] += dot_nt(act, down_ref[...])
    dn_ref[...] += dot_nt(grad_pre, up_ref[...])


def feed_forward(x1, a, b, gains, grad, up, down):
    rows, depth = x1.shape
    wide = up.shape[1]
    chunk = 384 if wide % 384 == 0 else wide
    shape = jax.ShapeDtypeStruct
    tall = pl.BlockSpec((depth, chunk), lambda i: (0, i))
    slab = pl.BlockSpec((rows, chunk), lambda i: (0, i))
    whole = full_block((rows, depth))
    return pl.pallas_call(
        feed_forward_kernel,
        grid=(wide // chunk,),
        in_specs=[whole, whole, whole, full_block(gains.shape), whole, tall, tall],
        out_specs=[whole, whole, slab, slab, whole, whole],
        out_shape=[
            shape((rows, depth), jnp.float32),
            shape((rows, depth), jnp.bfloat16),
            shape((rows, wide), jnp.bfloat16),
            shape((rows, wide), jnp.bfloat16),
            shape((rows, depth), jnp.float32),
            shape((rows, depth), jnp.float32),
        ],
        name="feed_forward",
        **params(8 * 10**9, 20 * 10**6),
    )(x1, a, b, gains, grad, up, down)


def attention_back_kernel(
    size, causal, gain_row, pieces, at_q, *refs,
):
    if causal:
        (x_ref, a_ref, b_ref, gain_ref, g_ref, q_ref, k_ref, v_ref, p_ref, rel_ref, *rest) = refs
    else:
        (x_ref, a_ref, b_ref, gain_ref, g_ref, q_ref, k_ref, v_ref, p_ref, *rest) = refs
    count = len({which for which, _, _ in pieces})
    weights, rest = rest[:count], rest[count:]
    if causal:
        sum_ref, low_ref, dgain_ref, dq_ref, dk_ref, dv_ref, table_ref, da_ref, diag_ref = rest
    else:
        sum_ref, low_ref, dgain_ref, dq_ref, dk_ref, dv_ref, dn_ref, da_ref = rest
    step = pl.program_id(0)

    @pl.when(step == 0)
    def _():
        add, dgain = norm_backward(x_ref[...], gain_ref[gain_row : gain_row + 1], a_ref[...] + b_ref[...])
        total = g_ref[...].astype(jnp.float32) + add
        sum_ref[...] = total
        total = low(total)
        low_ref[...] = total
        dgain_ref[...] = jnp.broadcast_to(dgain, dgain_ref.shape)
        at = 0
        for which, start, stop in pieces:
            da_ref[:, at : at + stop - start] = low(dot_nn(total, weights[which][:, start:stop]))
            at += stop - start

    lanes = group_lanes(step)
    if causal:
        diag_ref[...] = jnp.zeros_like(diag_ref)
    attend_back(
        q_ref[...], k_ref[...], v_ref[...], da_ref[:, lanes], p_ref,
        dq_ref if causal else dq_ref.at[:, lanes], dk_ref, dv_ref, diag_ref if causal else None, size,
    )
    if causal:
        by_bucket(diag_ref, rel_ref[...], table_ref, size)
    else:

        @pl.when(step == pl.num_programs(0) - 1)
        def _():
            part = dq_ref.shape[1]
            dn_ref[...] = dot_nt(dq_ref[...], weights[0][:, at_q : at_q + part])


def attention_back(x, a, b, gains, gain_row, grad, q, k, v, p, weights, pieces, at_q, rel_row, buckets, size):
    rows, depth = x.shape
    keys, part = k.shape
    causal = rel_row is not None
    pair = LANES // size
    groups = part // LANES
    shape = jax.ShapeDtypeStruct
    whole = full_block((rows, depth))
    tall = lambda count: pl.BlockSpec((count, LANES), lambda i: (0, i))
    in_specs = [
        whole,
        whole,
        whole,
        full_block(gains.shape),
        whole,
        tall(rows),
        tall(keys),
        tall(keys),
        pl.BlockSpec((pair, keys, rows), lambda i: (i, 0, 0)),
    ]
    args = [x, a, b, gains, grad, q, k, v, p]
    if causal:
        in_specs.append(full_block(rel_row.shape))
        args.append(rel_row)
    in_specs += [full_block(item.shape) for item in weights]
    args += list(weights)
    out_specs = [
        whole,
        whole,
        full_block((8, depth)),
        tall(rows) if causal else full_block((rows, part)),
        tall(keys),
        tall(keys),
    ]
    out_shape = [
        shape((rows, depth), jnp.float32),
        shape((rows, depth), jnp.bfloat16),
        shape((8, depth), jnp.float32),
        shape((rows, part), jnp.bfloat16),
        shape((keys, part), jnp.bfloat16),
        shape((keys, part), jnp.bfloat16),
    ]
    scratch = [pltpu.VMEM((rows, part), jnp.bfloat16)]
    if causal:
        out_specs.append(pl.BlockSpec((1, pair, buckets), lambda i: (i, 0, 0)))
        out_shape.append(shape((groups, pair, buckets), jnp.float32))
        scratch.append(pltpu.VMEM((pair, rel_row.shape[1] + LANES, LANES), jnp.float32))
    else:
        out_specs.append(whole)
        out_shape.append(shape((rows, depth), jnp.float32))
    return pl.pallas_call(
        functools.partial(attention_back_kernel, size, causal, gain_row, pieces, at_q),
        grid=(groups,),
        in_specs=in_specs,
        out_specs=out_specs,
        out_shape=out_shape,
        scratch_shapes=scratch,
        name="self_backward" if causal else "cross_backward",
        **params(12 * 10**9, 20 * 10**6),
    )(*args)


def split_grad_kernel(plan, place_ref, *refs):
    count = 1 + max(max(entry[1], entry[2]) for entry in plan)
    halves = 1 + max(entry[0] for entry in plan)
    inputs, outputs, (sum_ref, *flips) = refs[:count], refs[count : count + 2 * halves], refs[count + 2 * halves :]
    flipped = dict(zip(sorted({entry[1] for entry in plan}), flips))

    @pl.when(pl.program_id(0) == 0)
    def _():
        for left in flipped:
            flipped[left][...] = inputs[left][...].T

    for bit, left, right, first_row, start in plan:
        keep_ref, send_ref = outputs[2 * bit], outputs[2 * bit + 1]
        blocks, block_rows = keep_ref.shape[0], keep_ref.shape[1]
        mine = (place_ref[0] >> bit) & 1
        wide = inputs[right].shape[1]
        span = slice(start, start + wide)
        sum_ref[:, :wide] = low(dot_nn(flipped[left][:, first_row:], inputs[right][...]))
        for block in range(blocks):
            base = (block >> bit << (bit + 1)) | (block & ((1 << bit) - 1))
            kept = (base + (mine << bit)) * block_rows
            sent = (base + ((1 - mine) << bit)) * block_rows
            keep_ref[block, :, span] = sum_ref[pl.ds(pl.multiple_of(kept, 16), block_rows), :wide]
            send_ref[block, :, span] = sum_ref[pl.ds(pl.multiple_of(sent, 16), block_rows), :wide]


def split_grads(place, bits, inputs, plan, chunk=None):
    depth = inputs[plan[0][1]].shape[1]
    blocks = 1 << bits
    block_rows = depth // blocks
    wide = [sum(inputs[right].shape[1] for half, _, right, _, _ in plan if half == bit) for bit in (0, 1)]
    if block_rows % 16:
        found = []
        for bit in (0, 1):
            full = jnp.concatenate(
                [low(dot_tn(inputs[left][row:], inputs[right])) for half, left, right, row, _ in plan if half == bit],
                axis=1,
            ).reshape(1 << (bits - 1 - bit), 2, 1 << bit, block_rows, wide[bit])
            mine = (place >> bit) & 1
            found.append(
                tuple(
                    lax.dynamic_index_in_dim(full, index, 1, keepdims=False).reshape(-1, block_rows, wide[bit])
                    for index in (mine, 1 - mine)
                )
            )
        return found
    lefts = {left for _, left, _, _, _ in plan}
    out_specs, out_shape = [], []
    for bit in (0, 1):
        for _ in range(2):
            out_shape.append(jax.ShapeDtypeStruct((blocks // 2, block_rows, wide[bit]), jnp.bfloat16))
            out_specs.append(
                pl.BlockSpec((blocks // 2, block_rows, chunk or wide[bit]), lambda i: (0, 0, i if chunk else 0))
            )
    in_specs = [
        full_block(item.shape)
        if index in lefts or not chunk
        else pl.BlockSpec((item.shape[0], chunk), lambda i: (0, i))
        for index, item in enumerate(inputs)
    ]
    most = chunk or max(inputs[right].shape[1] for _, _, right, _, _ in plan)
    found = pl.pallas_call(
        functools.partial(split_grad_kernel, plan),
        grid=(wide[0] // chunk if chunk else 1,),
        in_specs=[pl.BlockSpec(memory_space=pltpu.SMEM)] + in_specs,
        out_specs=out_specs,
        out_shape=out_shape,
        scratch_shapes=[pltpu.VMEM((depth, most), jnp.bfloat16)]
        + [pltpu.VMEM(inputs[left].shape[::-1], jnp.bfloat16) for left in sorted(lefts)],
        name="split_grads",
        **params(4 * 10**9, 10 * 10**6),
    )(place.reshape(1), *inputs)
    return (found[0], found[1]), (found[2], found[3])


def input_grad_kernel(pieces, *refs):
    count = 1 + max(entry[0] for entry in pieces)
    tokens, refs = refs[:count], refs[count:]
    weights, out_ref = refs[:-1], refs[-1]
    total = None
    for which, start, stop, weight, at in pieces:
        term = dot_nt(tokens[which][:, start:stop], weights[weight][:, at : at + stop - start])
        total = term if total is None else total + term
    out_ref[...] = total


def input_grad(tokens, weights, pieces):
    rows = tokens[0].shape[0]
    depth = weights[0].shape[0]
    vmem = pl.BlockSpec(memory_space=pltpu.VMEM)
    return pl.pallas_call(
        functools.partial(input_grad_kernel, pieces),
        in_specs=[vmem] * (len(tokens) + len(weights)),
        out_specs=vmem,
        out_shape=jax.ShapeDtypeStruct((rows, depth), jnp.float32),
        name="input_grad",
        **params(1 * 10**9, 6 * 10**6),
    )(*tokens, *weights)


SEQ = ("far", "near")


def axis_bits(axis):
    return lax.axis_size(axis).bit_length() - 1


def partner_swap(value, axis, bit):
    count = lax.axis_size(axis)
    return lax.ppermute(value, axis, [(i, i ^ (1 << bit)) for i in range(count)])


def shifted(value, axis, steps):
    count = lax.axis_size(axis)
    leading, last = (max(0, -steps), min(count, count - steps))
    return lax.ppermute(value, axis, [(source, source + steps) for source in range(leading, last)])


def my_bit(axis, bit):
    return (lax.axis_index(axis) >> bit) & 1


def head_swap(value):
    return lax.ppermute(value, "heads", [(0, 1), (1, 0)])


def pin(value, *after):
    return lax.optimization_barrier((value, after))[0]


def joined(value, other, axis, bit, place):
    mine = my_bit(axis, bit) == 0
    return jnp.stack([jnp.where(mine, value, other), jnp.where(mine, other, value)], axis=place)


def gather_far(shard, axis):
    value = shard
    for place, bit in enumerate(range(axis_bits(axis) - 1, 1, -1)):
        value = joined(value, partner_swap(value, axis, bit), axis, bit, place)
    return value


def gather_near_first(value, axis, cut):
    place = axis_bits(axis) - 2
    left, right = value[..., :cut], value[..., cut:]
    return (
        joined(left, partner_swap(left, axis, 1), axis, 1, place),
        joined(right, partner_swap(right, axis, 0), axis, 0, place),
    )


def gather_near_last(halves, axis):
    left, right = halves
    place = axis_bits(axis) - 2
    left = joined(left, partner_swap(left, axis, 0), axis, 0, place + 1)
    right = joined(right, partner_swap(right, axis, 1), axis, 1, place)
    return tuple(item.reshape(-1, item.shape[-1]) for item in (left, right))


def keep_and_send(terms, axis, bit, place):
    mine = my_bit(axis, bit)
    keep, send = (
        sum(lax.dynamic_index_in_dim(term, index, place, keepdims=False).astype(jnp.float32) for term in terms)
        for index in (mine, 1 - mine)
    )
    return keep, low(send)


def near_last_parts(halves, axis):
    bits = axis_bits(axis)
    found = []
    for bit, terms in enumerate(halves):
        terms = [term.reshape((2,) * (bits - 1) + term.shape[-2:]) for term in terms]
        found.append(keep_and_send(terms, axis, 1 - bit, bits - 2))
    return found


def far_parts(terms, axis, bit):
    return keep_and_send(terms, axis, bit, terms[0].ndim - 3)


def send_far(parts, axis, bit):
    return parts[0], partner_swap(parts[1], axis, bit)


def columns(terms):
    return [jnp.concatenate(pieces, axis=-1) for pieces in zip(*terms)]


def sum_all(value, axis):
    for bit in range(axis_bits(axis)):
        value = value + partner_swap(value, axis, bit)
    return value


def matmul(spec, left, right):
    return jnp.einsum(spec, left, right, preferred_element_type=jnp.float32)


def block_before(value):
    rows = value.shape[-2] // 2
    core = lax.axis_index("heads")
    half = shifted(lax.dynamic_slice_in_dim(value, core * rows, rows, value.ndim - 2), SEQ, 1)
    other = head_swap(half)
    first = jnp.where(core == 0, half, other)
    second = jnp.where(core == 0, other, half)
    return first, second


def to_owner(part):
    rows = part.shape[0] // 2
    core = lax.axis_index("heads")
    mine = lax.dynamic_slice_in_dim(part, core * rows, rows)
    other = lax.dynamic_slice_in_dim(part, (1 - core) * rows, rows)
    return low(mine + head_swap(other))


def add_half(part, half):
    rows = half.shape[0]
    core = lax.axis_index("heads")
    half = half.astype(jnp.float32)
    blank = jnp.zeros_like(half)
    return part + jnp.concatenate([jnp.where(core == 0, half, blank), jnp.where(core == 0, blank, half)])


def per_device(
    hidden_in,
    memory,
    out_grad,
    norm_self,
    self_q,
    self_k,
    self_v,
    self_o,
    norm_cross,
    cross_q,
    cross_k,
    cross_v,
    cross_o,
    norm_ff,
    ff_in,
    ff_out,
    bias_table,
    seg_ids,
    mem_seg,
    rel_bucket,
):
    rows = hidden_in.shape[0]
    mem_rows = memory.shape[0]
    heads = bias_table.shape[1]
    buckets = bias_table.shape[0]
    part = self_q.shape[1]
    wide = ff_in.shape[1]
    size = part // heads
    bits = axis_bits(SEQ)
    position = lax.axis_index(SEQ)

    gains = jnp.pad(jnp.stack([norm_self, norm_cross, norm_ff], axis=1), ((0, 0), (0, LANES - 3)))
    first = gather_far(low(jnp.concatenate([self_q, self_k, gains, self_v], axis=1)), SEQ)
    before = block_before(jnp.stack([hidden_in, memory]))
    second = low(jnp.concatenate([cross_k, cross_v, self_o.T, cross_q, cross_o.T], axis=1))
    second = gather_far(pin(second, first), SEQ)
    cut_one = (2 * part + LANES + part) // 256 * 128
    first = gather_near_first(first, SEQ, cut_one)
    third = gather_far(pin(low(jnp.concatenate([ff_in, ff_out.T], axis=1)), second), SEQ)
    cut_two = 5 * part // 256 * 128
    second = gather_near_first(pin(second, first), SEQ, cut_two)
    first = gather_near_last(first, SEQ)

    def pair_of_blocks(ids, count):
        own = lax.dynamic_slice_in_dim(ids, position * count, count)
        prior = lax.dynamic_slice_in_dim(ids, jnp.maximum(position - 1, 0) * count, count)
        return jnp.concatenate([jnp.where(position > 0, prior, -2), own])

    seg_pair = pair_of_blocks(seg_ids, rows)
    mem_pair = pair_of_blocks(mem_seg, mem_rows)
    own_row = seg_pair[rows:].reshape(1, rows)
    seg_col = seg_pair.reshape(-1, 1)
    mem_col = mem_pair.reshape(-1, 1)
    rel_row = rel_bucket.reshape(1, -1)
    bias = bias_tiles(rel_row, bias_table)
    prior = jnp.concatenate([before[0][0], before[1][0]])
    mem_both = jnp.concatenate([before[0][1], before[1][1], memory])

    normed_pair, query_one, key_one, value_one, gain_rows = self_project(
        prior, hidden_in, first[0], first[1], part
    )
    query_one = pin(query_one, second)
    second = gather_near_last(second, SEQ)
    attend_one, weights_one = self_forward(
        query_one, key_one, value_one, seg_col, own_row, bias, size
    )
    third = gather_near_first(pin(third, second), SEQ, wide)
    more = cut_two - 2 * part
    rest = part - more
    left_two, right_two = second
    out_pieces = ((0, 2 * part, cut_two), (1, 0, rest))
    part_one = input_grad(
        [attend_one], [left_two, right_two], ((0, 0, more, 0, 2 * part), (0, more, part, 1, 0))
    )
    other_one = head_swap(part_one)
    mem_key, mem_value = (
        low(matmul("md,dw->mw", mem_both, left_two[:, at : at + part])) for at in (0, part)
    )

    mem_key = pin(mem_key, third)
    third = gather_near_last(third, SEQ)
    stream_one, normed_two, query_two, attend_two, weights_two, part_two = cross_forward(
        hidden_in, part_one, other_one, gain_rows, right_two, rest, rest + part, mem_key, mem_value,
        mem_col, own_row, size,
    )
    other_two = head_swap(part_two)

    stream_two, normed_three, active, grad_pre, part_three, back_three = feed_forward(
        stream_one, part_two, other_two, gain_rows, out_grad, third[0], third[1]
    )
    back_other = head_swap(back_three)
    other_three = head_swap(part_three)
    ff_split = split_grads(
        position, bits, (normed_three, grad_pre, out_grad, active),
        ((0, 0, 1, 0, 0), (1, 2, 3, 0, 0)), 384 if wide % 384 == 0 else None,
    )
    ff_terms = [(keep, partner_swap(send, SEQ, bit)) for bit, (keep, send) in enumerate(ff_split)]
    back_three, back_other = pin((back_three, back_other), ff_split)

    grad_two, low_two, gain_ff, grad_query_two, grad_mem_key, grad_mem_value, back_two = attention_back(
        stream_two, back_three, back_other, gain_rows, 2, out_grad, query_two, mem_key, mem_value,
        weights_two, [right_two], ((0, rest + part, rest + 2 * part),), rest, None, buckets, size,
    )
    other_back = head_swap(back_two)
    cross_split = split_grads(
        position, bits, (normed_two, grad_query_two, mem_both, grad_mem_key, grad_mem_value, low_two, attend_two),
        ((0, 0, 1, 0, 0), (0, 2, 3, 0, part), (1, 2, 4, 0, 0), (1, 5, 6, 0, part)),
    )
    cross_terms = [(keep, partner_swap(send, SEQ, bit)) for bit, (keep, send) in enumerate(cross_split)]
    mem_pieces = ((0, 0, part, 0, 0), (1, 0, part, 0, part))
    mem_back = input_grad([grad_mem_key[:mem_rows], grad_mem_value[:mem_rows]], [left_two], mem_pieces)
    mem_back = to_owner(mem_back)
    mem_came = shifted(mem_back, SEQ, -1)
    ff_terms = [(keep, pin(got, mem_back)) for keep, got in ff_terms]
    ff_parts = near_last_parts(ff_terms, SEQ)
    ff_terms = [(keep, partner_swap(send, SEQ, 1 - bit)) for bit, (keep, send) in enumerate(ff_parts)]
    back_two, other_back = pin((back_two, other_back), cross_split, ff_parts, mem_back)

    grad_one, low_one, gain_cross, grad_query_one, grad_key_one, grad_value_one, table_part = attention_back(
        stream_one, back_two, other_back, gain_rows, 1, grad_two, query_one, key_one, value_one,
        weights_one, [left_two, right_two], out_pieces, None, rel_row, buckets, size,
    )
    self_split = split_grads(
        position, bits, (normed_pair, grad_query_one, grad_key_one, grad_value_one, low_one, attend_one),
        ((0, 0, 1, rows, 0), (0, 0, 2, 0, part), (1, 0, 3, 0, 0), (1, 4, 5, 0, part)),
    )
    ff_terms = [(keep, pin(got, grad_query_one)) for keep, got in ff_terms]
    cross_terms = [(keep, pin(got, grad_query_one)) for keep, got in cross_terms]
    ff_parts = far_parts(columns(ff_terms), SEQ, 2)
    ff_terms = send_far(ff_parts, SEQ, 2)
    cross_parts = near_last_parts(cross_terms, SEQ)
    cross_terms = [(keep, partner_swap(send, SEQ, 1 - bit)) for bit, (keep, send) in enumerate(cross_parts)]
    self_terms = [(keep, partner_swap(send, SEQ, bit)) for bit, (keep, send) in enumerate(self_split)]

    more_one = cut_one - part
    rest_one = part - more_one
    key_pieces = ((0, 0, more_one, 0, part), (0, more_one, part, 1, 0), (1, 0, part, 1, rest_one + LANES))
    own_pieces = key_pieces + ((2, 0, part, 0, 0),)
    grad_key_one, grad_value_one = pin((grad_key_one, grad_value_one), self_split)
    self_back = to_owner(input_grad([grad_key_one[:rows], grad_value_one[:rows]], list(first), key_pieces))
    self_came = shifted(self_back, SEQ, -1)
    self_part = input_grad(
        [grad_key_one[rows:], grad_value_one[rows:], grad_query_one], list(first), own_pieces
    )
    mem_part = input_grad([grad_mem_key[mem_rows:], grad_mem_value[mem_rows:]], [left_two], mem_pieces)
    mem_part = add_half(mem_part, pin(mem_came, self_back))
    grad_memory = mem_part + head_swap(mem_part)
    self_part = add_half(self_part, self_came)
    grad_normed = self_part + head_swap(self_part)
    add, gain_self = norm_backward(hidden_in.astype(jnp.float32), gain_rows[0:1], grad_normed)
    grad_hidden = grad_one + add

    for bit in range(3, bits):
        ff_terms = send_far(far_parts(ff_terms, SEQ, bit), SEQ, bit)
    cross_terms = columns(cross_terms)
    for bit in range(2, bits):
        cross_terms = send_far(far_parts(cross_terms, SEQ, bit), SEQ, bit)
    self_parts = near_last_parts(self_terms, SEQ)
    self_terms = [(keep, partner_swap(send, SEQ, 1 - bit)) for bit, (keep, send) in enumerate(self_parts)]
    self_terms = columns(self_terms)
    for bit in range(2, bits):
        self_terms = send_far(far_parts(self_terms, SEQ, bit), SEQ, bit)
    gain_grads = jnp.stack([gain_self[0], gain_cross[0], gain_ff[0]], axis=1)
    gain_terms = [jnp.pad(gain_grads, ((0, 0), (0, LANES - 3))).reshape((2,) * bits + (-1, LANES))]
    for bit in range(bits):
        gain_terms = send_far(far_parts(gain_terms, SEQ, bit), SEQ, bit)
    grad_table = sum_all(table_part.reshape(heads, -1).T, SEQ)
    ff_summed, cross_summed, self_summed, gain_summed = (
        keep + got.astype(jnp.float32) for keep, got in (ff_terms, cross_terms, self_terms, gain_terms)
    )
    return (
        low(stream_two + (part_three + other_three)),
        grad_hidden,
        grad_memory,
        gain_summed[:, 0],
        self_summed[:, :part],
        self_summed[:, part : 2 * part],
        self_summed[:, 2 * part : 3 * part],
        self_summed[:, 3 * part :].T,
        gain_summed[:, 1],
        cross_summed[:, :part],
        cross_summed[:, part : 2 * part],
        cross_summed[:, 2 * part : 3 * part],
        cross_summed[:, 3 * part :].T,
        gain_summed[:, 2],
        ff_summed[:, :wide],
        ff_summed[:, wide:].T,
        grad_table,
    )


def solution(mesh):
    count = mesh.shape["seq"]
    near = min(4, count)
    grid = Mesh(mesh.devices.reshape(count // near, near, -1), SEQ + ("heads",))
    in_specs = (
        P(SEQ, None),
        P(SEQ, None),
        P(SEQ, None),
        P(SEQ),
        P(SEQ, "heads"),
        P(SEQ, "heads"),
        P(SEQ, "heads"),
        P("heads", SEQ),
        P(SEQ),
        P(SEQ, "heads"),
        P(SEQ, "heads"),
        P(SEQ, "heads"),
        P("heads", SEQ),
        P(SEQ),
        P(SEQ, "heads"),
        P("heads", SEQ),
        P(None, "heads"),
        P(),
        P(),
        P(),
    )
    out_specs = (
        P(SEQ, None),
        P(SEQ, None),
        P(SEQ, None),
        P(SEQ),
        P(SEQ, "heads"),
        P(SEQ, "heads"),
        P(SEQ, "heads"),
        P("heads", SEQ),
        P(SEQ),
        P(SEQ, "heads"),
        P(SEQ, "heads"),
        P(SEQ, "heads"),
        P("heads", SEQ),
        P(SEQ),
        P(SEQ, "heads"),
        P("heads", SEQ),
        P(None, "heads"),
    )
    return jax.shard_map(
        per_device, mesh=grid, in_specs=in_specs, out_specs=out_specs, check_vma=False
    )
```

time: 2090 us -> 403 us (0.19)
  waiting for transfers between devices: 1350 us -> 95.2 us
  blocking collectives: 447 us -> 0 us
  matrix products: 165 us -> 3.71 us
  Pallas kernels: 0 us -> 132 us
  starting transfers between devices: 17.8 us -> 87.3 us
  other arithmetic: 57.6 us -> 33 us
    reduce_scatter x8 -> x0, waiting for transfers between devices: 930 us -> none  [the longest x1 143 us: per_device(): lax.psum_scatter(grad_down, 'seq', scatter_dimension=1, tiled=True)]
    all_gather x8 -> x0, blocking collectives: 341 us -> none  [the longest x1 44.4 us: per_device(): lax.all_gather(self_v.astype(low_type), 'seq', axis=0, tiled=True)]
    unnamed x19 -> x0, waiting for transfers between devices: 258 us -> none
    dot_general x43 -> x2, matrix products: 138 us -> 3.71 us  [matmul(): return jnp.einsum(spec, left, right, preferred_element_type=jnp.float32)]
    pallas_call x0 -> x15, Pallas kernels: none -> 132 us  [the longest x2 37.7 us: attention_back(): pl.pallas_call(functools.partial(attention_back_kernel, size, causal, gai...]
    unnamed x2 -> x0, blocking collectives: 106 us -> none
    all_gather x2 -> x0, waiting for transfers between devices: 101 us -> none  [the longest x1 59.1 us: per_device(): lax.all_gather(ff_in.astype(low_type), 'seq', axis=0, tiled=True)]
    ppermute x0 -> x54, waiting for transfers between devices: none -> 85.4 us  [the longest x44 85.4 us: partner_swap(): return lax.ppermute(value, axis, [(i, i ^ 1 << bit) for i in range(count)])]
  transfers between devices with their start and end apart: 25 -> 57, of which waited for: 19 -> 20; matrix products, arithmetic and copies ran while one was open for 6% -> 18% of each run, Pallas kernels for 0% -> 29%
where the time goes in v2:
time: 403 us; the launch traced here: 396 us
  Pallas kernels  132 us (33%)
  waiting for transfers between devices  95.2 us (24%)
  starting transfers between devices  87.3 us (22%)
  local copies, waits for them, and re-layouts  42.7 us (11%)
  other arithmetic  33 us (8%)
    ppermute x44, waiting for transfers between devices, partner_swap(): return lax.ppermute(value, axis, [(i, i ^ 1 << bit) for i in range(count)])  85.4 us
    ppermute x44, starting transfers between devices, partner_swap(): return lax.ppermute(value, axis, [(i, i ^ 1 << bit) for i in range(count)])  75.9 us
    pallas_call x2, Pallas kernels, attention_back(): pl.pallas_call(functools.partial(attention_back_kernel, size, causal, gai...  37.7 us
    pallas_call x3, Pallas kernels, split_grads(): pl.pallas_call(functools.partial(split_grad_kernel, plan), grid=(wide[0]...  22 us
    pallas_call x5, Pallas kernels, input_grad(): pl.pallas_call(functools.partial(input_grad_kernel, pieces), in_specs=[vm...  19.7 us
    pallas_call x1, Pallas kernels, cross_forward(): pl.pallas_call(functools.partial(cross_forward_kernel, size, at_q, at_o),...  18.3 us
    pallas_call x1, Pallas kernels, self_forward(): pl.pallas_call(functools.partial(self_forward_kernel, size), grid=(part /...  13 us
    pallas_call x1, Pallas kernels, feed_forward(): pl.pallas_call(feed_forward_kernel, grid=(wide // chunk,), in_specs=[whol...  12.9 us
  transfers between devices with their start and end apart: 57, of which 20 were waited for; matrix products, arithmetic and copies ran while one was open for 18% of the time, Pallas kernels for 29%

profile of v2, /device:TPU:2, one launch (start us, length us, event | category | flops | bytes accessed | tf_op | source)
XLA Modules:
  0.0 396.5 jit_solution(6527727899388839414)
XLA Ops:
  13.5 3.6 bias_tiles.1.bias_ref
  22.9 5.4 %collective-permute-done.3 = bf16[2,48,1280]{2,1,0:T(8,128)(2,1)S(1)} collective-permute-done((bf16[2,48,1280]{2,1,0:T(8,128)(2,1)S(1)}, bf16[2,48,1280]{2,1,0:T(8,128)(2,1)S(1)}, u32[]{:S(2)}, u32[]{:S(2)}) %collective-permute-start.3) | collective-permute-done | bytes 245792 | tf_op jit(solution)/shard_map/ppermute | solution.py:619
  28.5 13.3 %collective-permute-start.4 = (bf16[2,2,48,640]{3,2,0,1:T(8,128)(2,1)S(1)}, bf16[2,2,48,640]{3,2,0,1:T(8,128)(2,1)S(1)}, u32[]{:S(2)}, u32[]{:S(2)}) collective-permute-start(bf16[2,2,48,640]{3,2,0,1:T(8,128)(2,1)S(1)} %get-tuple-element.231), channel_id=1, source_target_pairs={{0,4},{2,6},{4,0},{6,2},{8,12},{10,14},{12,8},{14,10},{16,20},{18,... | collective-permute-start | bytes 737288 | tf_op jit(solution)/shard_map/ppermute | solution.py:619
  42.0 4.1 %collective-permute-start.15 = (bf16[48,3072]{1,0:T(8,128)(2,1)S(1)}, bf16[48,3072]{1,0:T(8,128)(2,1)S(1)}, u32[]{:S(2)}, u32[]{:S(2)}) collective-permute-start(bf16[48,3072]{1,0:T(8,128)(2,1)S(1)} %pad_maximum_fusion.19), channel_id=1, source_target_pairs={{0,16},{2,18},{4,20},{6,22},{8,24},{10,26},{12,28},{14,30},{16,0},... | collective-permute-start | bytes 884744 | tf_op jit(solution)/shard_map/ppermute | solution.py:619
  49.6 3.7 collective-permute-start.7
  57.6 13.3 %collective-permute-done.10 = bf16[2,2,48,896]{3,2,0,1:T(8,128)(2,1)S(1)} collective-permute-done((bf16[2,2,48,896]{3,2,0,1:T(8,128)(2,1)S(1)}, bf16[2,2,48,896]{3,2,0,1:T(8,128)(2,1)S(1)}, u32[]{:S(2)}, u32[]{:S(2)}) %collective-permute-start.10) | collective-permute-done | bytes 344096 | tf_op jit(solution)/shard_map/ppermute | solution.py:619
  80.7 4.4 %collective-permute-done.16 = bf16[2,48,3072]{2,1,0:T(8,128)(2,1)S(1)} collective-permute-done((bf16[2,48,3072]{2,1,0:T(8,128)(2,1)S(1)}, bf16[2,48,3072]{2,1,0:T(8,128)(2,1)S(1)}, u32[]{:S(2)}, u32[]{:S(2)}) %collective-permute-start.16) | collective-permute-done | bytes 589856 | tf_op jit(solution)/shard_map/ppermute | solution.py:619
  86.5 5.3 %self_project.1 = (bf16[1024,768]{1,0:T(8,128)(2,1)}, bf16[512,384]{1,0:T(8,128)(2,1)}, bf16[1024,384]{1,0:T(8,128)(2,1)}, bf16[1024,384]{1,0:T(8,128)(2,1)}, f32[8,768]{1,0:T(8,128)}) custom-call(bf16[512,768]{1,0:T(8,128)(2,1)} %pad_maximum_fusion.10.prior_ref, bf16[512,768]{1,0:T(8,128)(2,1)} %x_ref.1, bf16[768,640]{1,0:T(8,128)(2,1)} %bitcast.240, ...), custom_call_target="tpu_custom_call" | custom-call | flops 4000000000 | bytes 10000000 | tf_op jit(solution)/shard_map/self_project/pallas_call | solution.py:238
  91.8 13.0 %self_forward.1 = (bf16[512,384]{1,0:T(8,128)(2,1)}, bf16[6,1024,512]{2,1,0:T(8,128)(2,1)}) custom-call(bf16[512,384]{1,0:T(8,128)(2,1)} %get-tuple-element.84.q_ref.refs_5_, bf16[1024,384]{1,0:T(8,128)(2,1)} %get-tuple-element.85.k_ref.refs_6_, bf16[1024,384]{1,0:T(8,128)(2,1)} %get-tuple-element.86.v_ref.refs_7_, s32[1024,1]{1,0:T(8,128)} %copy.106.seg_ref, ...), custom_call_target="tpu_custom_call" | custom-call | flops 12000000000 | bytes 20000000 | tf_op jit(solution)/shard_map/self_forward/pallas_call | solution.py:265
  110.1 3.7 input_grad.5.a_ref
  120.7 9.1 %collective-permute-done.18 = bf16[2,2,48,1536]{3,2,0,1:T(8,128)(2,1)S(1)} collective-permute-done((bf16[2,2,48,1536]{3,2,0,1:T(8,128)(2,1)S(1)}, bf16[2,2,48,1536]{3,2,0,1:T(8,128)(2,1)S(1)}, u32[]{:S(2)}, u32[]{:S(2)}) %collective-permute-start.18) | collective-permute-done | bytes 589856 | tf_op jit(solution)/shard_map/ppermute | solution.py:619
  134.5 18.3 %cross_forward.1 = (f32[512,768]{1,0:T(8,128)}, bf16[512,768]{1,0:T(8,128)(2,1)}, bf16[512,384]{1,0:T(8,128)(2,1)}, bf16[512,384]{1,0:T(8,128)(2,1)}, bf16[6,1024,512]{2,1,0:T(8,128)(2,1)}, /*index=5*/f32[512,768]{1,0:T(8,128)}) custom-call(bf16[512,768]{1,0:T(8,128)(2,1)} %x_ref.1, f32[512,768]{1,0:T(8,128)} %input_grad.5.a_ref, ...), custom_call_target="tpu_custom_call" | custom-call | flops 12000000000 | bytes 20000000 | tf_op jit(solution)/shard_map/cross_forward/pallas_call | solution.py:315
  152.9 5.7 %collective-permute-done.20 = bf16[2,2,2,48,1536]{4,3,0,1,2:T(8,128)(2,1)S(1)} collective-permute-done((bf16[2,2,2,48,1536]{4,3,0,1,2:T(8,128)(2,1)S(1)}, bf16[2,2,2,48,1536]{4,3,0,1,2:T(8,128)(2,1)S(1)}, u32[]{:S(2)}, u32[]{:S(2)}) %collective-permute-start.20) | collective-permute-done | bytes 1179680 | tf_op jit(solution)/shard_map/ppermute | solution.py:619
  163.7 12.9 %feed_forward.1 = (f32[512,768]{1,0:T(8,128)}, bf16[512,768]{1,0:T(8,128)(2,1)}, bf16[512,1536]{1,0:T(8,128)(2,1)}, bf16[512,1536]{1,0:T(8,128)(2,1)}, f32[512,768]{1,0:T(8,128)}, /*index=5*/f32[512,768]{1,0:T(8,128)}) custom-call(f32[512,768]{1,0:T(8,128)} %get-tuple-element.92.x1_ref.refs_0_, f32[512,768]{1,0:T(8,128)} %get-tuple-element.93.a_ref, ...), custom_call_target="tpu_custom_call" | custom-call | flops 8000000000 | bytes 20000000 | tf_op jit(solution)/shard_map/feed_forward/pallas_call | solution.py:385
  179.5 8.1 %split_grads.3 = (bf16[8,48,1536]{2,1,0:T(8,128)(2,1)}, bf16[8,48,1536]{2,1,0:T(8,128)(2,1)}, bf16[8,48,1536]{2,1,0:T(8,128)(2,1)}, bf16[8,48,1536]{2,1,0:T(8,128)(2,1)}) custom-call(s32[1]{0:T(128)} %bitcast.59.place_ref, bf16[512,768]{1,0:T(8,128)(2,1)} %get-tuple-element.97.refs_0_, bf16[512,1536]{1,0:T(8,128)(2,1)} %get-tuple-element.98.refs_1_, ...), custom_call_target="tpu_custom_call" | custom-call | flops 4000000000 | bytes 10000000 | tf_op jit(solution)/shard_map/split_grads/pallas_call | solution.py:571
  191.6 19.7 %cross_backward.1 = (f32[512,768]{1,0:T(8,128)}, bf16[512,768]{1,0:T(8,128)(2,1)}, f32[8,768]{1,0:T(8,128)}, bf16[512,384]{1,0:T(8,128)(2,1)}, bf16[1024,384]{1,...) custom-call(f32[512,768]{1,0:T(8,128)} %get-tuple-element.94.refs_0_, ...), custom_call_target="tpu_custom_call" | custom-call | flops 12000000000 | bytes 20000000 | tf_op jit(solution)/shard_map/cross_backward/pallas_call | solution.py:498
  214.5 3.7 input_grad.6
  220.7 7.1 %split_grads.4 = (bf16[8,48,768]{2,1,0:T(8,128)(2,1)}, bf16[8,48,768]{2,1,0:T(8,128)(2,1)}, bf16[8,48,768]{2,1,0:T(8,128)(2,1)}, bf16[8,48,768]{2,1,0:T(8,128)(2,1)}) custom-call(s32[1]{0:T(128)} %bitcast.59.place_ref, bf16[512,768]{1,0:T(8,128)(2,1)} %get-tuple-element.109.refs_0_, bf16[512,384]{1,0:T(8,128)(2,1)} %get-tuple-element.110.refs_1_, ...), custom_call_target="tpu_custom_call" | custom-call | flops 4000000000 | bytes 10000000 | tf_op jit(solution)/shard_map/split_grads/pallas_call | solution.py:571
  230.5 3.9 input_grad.9
  249.6 18.0 %self_backward.1 = (f32[512,768]{1,0:T(8,128)}, bf16[512,768]{1,0:T(8,128)(2,1)}, f32[8,768]{1,0:T(8,128)}, bf16[512,384]{1,0:T(8,128)(2,1)}, bf16[1024,384]{1,0...) custom-call(f32[512,768]{1,0:T(8,128)} %get-tuple-element.92.x1_ref.refs_0_, ...), custom_call_target="tpu_custom_call" | custom-call | flops 12000000000 | bytes 20000000 | tf_op jit(solution)/shard_map/self_backward/pallas_call | solution.py:498
  267.5 6.9 %split_grads.5 = (bf16[8,48,768]{2,1,0:T(8,128)(2,1)}, bf16[8,48,768]{2,1,0:T(8,128)(2,1)}, bf16[8,48,768]{2,1,0:T(8,128)(2,1)}, bf16[8,48,768]{2,1,0:T(8,128)(2,1)}) custom-call(s32[1]{0:T(128)} %bitcast.59.place_ref, bf16[1024,768]{1,0:T(8,128)(2,1)} %get-tuple-element.128.refs_0_, bf16[512,384]{1,0:T(8,128)(2,1)} %get-tuple-element.129.refs_1_.refs_2_, ...), custom_call_target="tpu_custom_call" | custom-call | flops 4000000000 | bytes 10000000 | tf_op jit(solution)/shard_map/split_grads/pallas_call | solution.py:571
  288.6 3.9 input_grad.8
  298.5 4.1 %collective-permute-done.46 = bf16[2,2,48,768]{3,2,0,1:T(8,128)(2,1)S(1)} collective-permute-done((bf16[2,2,48,768]{3,2,0,1:T(8,128)(2,1)S(1)}, bf16[2,2,48,768]{3,2,0,1:T(8,128)(2,1)S(1)}, u32[]{:S(2)}, u32[]{:S(2)}) %collective-permute-start.46) | collective-permute-done | bytes 294944 | tf_op jit(solution)/shard_map/ppermute | solution.py:619
  305.0 4.6 %collective-permute-done.55 = f32[32,6]{0,1:T(8,128)S(1)} collective-permute-done((f32[32,6]{0,1:T(8,128)S(1)}, f32[32,6]{0,1:T(8,128)S(1)}, u32[]{:S(2)}, u32[]{:S(2)}) %collective-permute-start.55) | collective-permute-done | bytes 800 | tf_op jit(solution)/shard_map/ppermute | solution.py:619
  311.8 4.4 %input_grad.7 = f32[512,768]{1,0:T(8,128)} custom-call(bf16[512,384]{1,0:T(8,128)(2,1)} %get-tuple-element.199.refs_0_, bf16[512,384]{1,0:T(8,128)(2,1)} %get-tuple-element.197.refs_1_, bf16[512,384]{1,0:T(8,128)(2,1)} %get-tuple-element.129.refs_1_.refs_2_, bf16[768,640]{1,0:T(8,128)(2,1)} %bitcast.242, bf16[768,640]{1,0:T(8,128)(2,1)} %bitcast.245), custom_call_target="tpu_custom_call" | custom-call | flops 1000000000 | bytes 6000000 | tf_op jit(solution)/shard_map/input_grad/pallas_call | solution.py:600
  323.1 12.6 %collective-permute-done.51 = bf16[2,48,3072]{2,1,0:T(8,128)(2,1)S(1)} collective-permute-done((bf16[2,48,3072]{2,1,0:T(8,128)(2,1)S(1)}, bf16[2,48,3072]{2,1,0:T(8,128)(2,1)S(1)}, u32[]{:S(2)}, u32[]{:S(2)}) %collective-permute-start.51) | collective-permute-done | bytes 589856 | tf_op jit(solution)/shard_map/ppermute | solution.py:619
  337.9 3.8 collective-permute-start.29
  344.4 9.7 %collective-permute-done.29 = bf16[256,768]{1,0:T(8,128)(2,1)S(1)} collective-permute-done((bf16[256,768]{1,0:T(8,128)(2,1)S(1)}, bf16[256,768]{1,0:T(8,128)(2,1)S(1)}, u32[]{:S(2)}, u32[]{:S(2)}) %collective-permute-start.29) | collective-permute-done | bytes 393248 | tf_op jit(solution)/shard_map/ppermute | solution.py:625
  355.8 8.4 %collective-permute-done.41 = bf16[2,48,1536]{2,1,0:T(8,128)(2,1)S(1)} collective-permute-done((bf16[2,48,1536]{2,1,0:T(8,128)(2,1)S(1)}, bf16[2,48,1536]{2,1,0:T(8,128)(2,1)S(1)}, u32[]{:S(2)}, u32[]{:S(2)}) %collective-permute-start.41) | collective-permute-done | bytes 294944 | tf_op jit(solution)/shard_map/ppermute | solution.py:619
  366.4 6.8 %collective-permute-start.33 = (bf16[2,2,2,48,128]{4,3,2,1,0:T(8,128)(2,1)S(1)}, bf16[2,2,2,48,128]{4,3,2,1,0:T(8,128)(2,1)S(1)}, u32[]{:S(2)}, u32[]{:S(2)}) collective-permute-start(bf16[2,2,2,48,128]{4,3,2,1,0:T(8,128)(2,1)S(1)} %fusion.48), channel_id=1, source_target_pairs={{0,2},{2,0},{4,6},{6,4},{8,10},{10,8},{12,14},{14,12},{16,18},{18,... | collective-permute-start | bytes 294920 | tf_op jit(solution)/shard_map/ppermute | solution.py:619
  375.8 7.1 %collective-permute-start.34 = (bf16[2,2,48,128]{3,2,1,0:T(8,128)(2,1)S(1)}, bf16[2,2,48,128]{3,2,1,0:T(8,128)(2,1)S(1)}, u32[]{:S(2)}, u32[]{:S(2)}) collective-permute-start(bf16[2,2,48,128]{3,2,1,0:T(8,128)(2,1)S(1)} %get-tuple-element.226), channel_id=1, source_target_pairs={{0,4},{2,6},{4,0},{6,2},{8,12},{10,14},{12,8},{14,10},{16,20},{18,... | collective-permute-start | bytes 147464 | tf_op jit(solution)/shard_map/ppermute | solution.py:619
  387.1 3.8 collective-permute-done.35
  (341 shorter events, 141.7 us)
Async XLA Ops:
  2.1 51.3 %collective-permute-start = (bf16[2,256,768]{2,1,0:T(8,128)(2,1)S(1)}, bf16[2,256,768]{2,1,0:T(8,128)(2,1)S(1)}, u32[]{:S(2)}, u32[]{:S(2)}) collective-permute-start(bf16[2,256,768]{2,1,0:T(8,128)(2,1)S(1)} %fusion.14), channel_id=1, source_target_pairs={{0,2},{2,4},{4,6},{6,8},{8,10},{10,12},{12,14},{14,16},{16,18},{18... | collective-permute-start | bytes 2359304 | tf_op jit(solution)/shard_map/ppermute | solution.py:625
  22.3 19.5 %collective-permute-start.9 = (bf16[2,48,1920]{2,1,0:T(8,128)(2,1)S(1)}, bf16[2,48,1920]{2,1,0:T(8,128)(2,1)S(1)}, u32[]{:S(2)}, u32[]{:S(2)}) collective-permute-start(bf16[2,48,1920]{2,1,0:T(8,128)(2,1)S(1)} %pad_maximum_fusion.18), channel_id=1, source_target_pairs={{0,8},{2,10},{4,12},{6,14},{8,0},{10,2},{12,4},{14,6},{16,24},{18,... | collective-permute-start | bytes 1105928 | tf_op jit(solution)/shard_map/ppermute | solution.py:619
  28.5 17.7 %collective-permute-start.4 = (bf16[2,2,48,640]{3,2,0,1:T(8,128)(2,1)S(1)}, bf16[2,2,48,640]{3,2,0,1:T(8,128)(2,1)S(1)}, u32[]{:S(2)}, u32[]{:S(2)}) collective-permute-start(bf16[2,2,48,640]{3,2,0,1:T(8,128)(2,1)S(1)} %get-tuple-element.231), channel_id=1, source_target_pairs={{0,4},{2,6},{4,0},{6,2},{8,12},{10,14},{12,8},{14,10},{16,20},{18,... | collective-permute-start | bytes 737288 | tf_op jit(solution)/shard_map/ppermute | solution.py:619
  46.3 30.0 %collective-permute-start.5 = (bf16[2,2,2,48,640]{4,3,0,1,2:T(8,128)(2,1)S(1)}, bf16[2,2,2,48,640]{4,3,0,1,2:T(8,128)(2,1)S(1)}, u32[]{:S(2)}, u32[]{:S(2)}) collective-permute-start(bf16[2,2,2,48,640]{4,3,0,1,2:T(8,128)(2,1)S(1)} %pad_maximum_fusion.16), channel_id=1, source_target_pairs={{0,2},{2,0},{4,6},{6,4},{8,10},{10,8},{12,14},{14,12},{16,18},{18,... | collective-permute-start | bytes 1474568 | tf_op jit(solution)/shard_map/ppermute | solution.py:619
  49.6 29.8 %collective-permute-start.7 = (bf16[2,2,2,48,640]{4,3,0,1,2:T(8,128)(2,1)S(1)}, bf16[2,2,2,48,640]{4,3,0,1,2:T(8,128)(2,1)S(1)}, u32[]{:S(2)}, u32[]{:S(2)}) collective-permute-start(bf16[2,2,2,48,640]{4,3,0,1,2:T(8,128)(2,1)S(1)} %pad_maximum_fusion.17), channel_id=1, source_target_pairs={{0,4},{2,6},{4,0},{6,2},{8,12},{10,14},{12,8},{14,10},{16,20},{18,... | collective-permute-start | bytes 1474568 | tf_op jit(solution)/shard_map/ppermute | solution.py:619
  53.4 17.5 %collective-permute-start.10 = (bf16[2,2,48,896]{3,2,0,1:T(8,128)(2,1)S(1)}, bf16[2,2,48,896]{3,2,0,1:T(8,128)(2,1)S(1)}, u32[]{:S(2)}, u32[]{:S(2)}) collective-permute-start(bf16[2,2,48,896]{3,2,0,1:T(8,128)(2,1)S(1)} %slice.112), channel_id=1, source_target_pairs={{0,4},{2,6},{4,0},{6,2},{8,12},{10,14},{12,8},{14,10},{16,20},{18,... | collective-permute-start | bytes 1032200 | tf_op jit(solution)/shard_map/ppermute | solution.py:619
  53.5 20.9 %collective-permute-start.11 = (bf16[2,2,48,1024]{3,2,0,1:T(8,128)(2,1)S(1)}, bf16[2,2,48,1024]{3,2,0,1:T(8,128)(2,1)S(1)}, u32[]{:S(2)}, u32[]{:S(2)}) collective-permute-start(bf16[2,2,48,1024]{3,2,0,1:T(8,128)(2,1)S(1)} %slice.113), channel_id=1, source_target_pairs={{0,2},{2,0},{4,6},{6,4},{8,10},{10,8},{12,14},{14,12},{16,18},{18,... | collective-permute-start | bytes 1179656 | tf_op jit(solution)/shard_map/ppermute | solution.py:619
  57.5 27.8 %collective-permute-start.1 = (bf16[2,256,768]{2,1,0:T(8,128)(2,1)S(1)}, bf16[2,256,768]{2,1,0:T(8,128)(2,1)S(1)}, u32[]{:S(2)}, u32[]{:S(2)}) collective-permute-start(bf16[2,256,768]{2,1,0:T(8,128)(2,1)S(1)} %collective-permute-done), channel_id=1, source_target_pairs={{0,1},{1,0},{2,3},{3,2},{4,5},{5,4},{6,7},{7,6},{8,9},{9,8},{10,11... | collective-permute-start | bytes 2359304 | tf_op jit(solution)/shard_map/ppermute | solution.py:633
  74.4 30.4 %collective-permute-start.12 = (bf16[2,2,2,48,896]{4,3,0,1,2:T(8,128)(2,1)}, bf16[2,2,2,48,896]{4,3,0,1,2:T(8,128)(2,1)}, u32[]{:S(2)}, u32[]{:S(2)}) collective-permute-start(bf16[2,2,2,48,896]{4,3,0,1,2:T(8,128)(2,1)} %pad_maximum_fusion.13), channel_id=1, source_target_pairs={{0,2},{2,0},{4,6},{6,4},{8,10},{10,8},{12,14},{14,12},{16,18},{18,... | collective-permute-start | bytes 2064392 | tf_op jit(solution)/shard_map/ppermute | solution.py:619
  76.3 31.2 %collective-permute-start.13 = (bf16[2,2,2,48,1024]{4,3,0,1,2:T(8,128)(2,1)S(1)}, bf16[2,2,2,48,1024]{4,3,0,1,2:T(8,128)(2,1)}, u32[]{:S(2)}, u32[]{:S(2)}) collective-permute-start(bf16[2,2,2,48,1024]{4,3,0,1,2:T(8,128)(2,1)S(1)} %pad_maximum_fusion.11), channel_id=1, source_target_pairs={{0,4},{2,6},{4,0},{6,2},{8,12},{10,14},{12,8},{14,10},{16,20},{18,... | collective-permute-start | bytes 2359304 | tf_op jit(solution)/shard_map/ppermute | solution.py:619
  113.9 20.6 %collective-permute-start.14 = (f32[512,768]{1,0:T(8,128)}, f32[512,768]{1,0:T(8,128)}, u32[]{:S(2)}, u32[]{:S(2)}) collective-permute-start(f32[512,768]{1,0:T(8,128)} %input_grad.5.a_ref), channel_id=1, source_target_pairs={{0,1},{1,0},{2,3},{3,2},{4,5},{5,4},{6,7},{7,6},{8,9},{9,8},{10,11... | collective-permute-start | bytes 4718600 | tf_op jit(solution)/shard_map/ppermute | solution.py:633
  131.2 27.3 %collective-permute-start.20 = (bf16[2,2,2,48,1536]{4,3,0,1,2:T(8,128)(2,1)S(1)}, bf16[2,2,2,48,1536]{4,3,0,1,2:T(8,128)(2,1)S(1)}, u32[]{:S(2)}, u32[]{:S(2)}) collective-permute-start(bf16[2,2,2,48,1536]{4,3,0,1,2:T(8,128)(2,1)S(1)} %pad_maximum_fusion.6), channel_id=1, source_target_pairs={{0,2},{2,0},{4,6},{6,4},{8,10},{10,8},{12,14},{14,12},{16,18},{18,... | collective-permute-start | bytes 3538952 | tf_op jit(solution)/shard_map/ppermute | solution.py:619
  133.0 27.5 %collective-permute-start.21 = (bf16[2,2,2,48,1536]{4,3,0,1,2:T(8,128)(2,1)}, bf16[2,2,2,48,1536]{4,3,0,1,2:T(8,128)(2,1)S(1)}, u32[]{:S(2)}, u32[]{:S(2)}) collective-permute-start(bf16[2,2,2,48,1536]{4,3,0,1,2:T(8,128)(2,1)} %pad_maximum_fusion.7), channel_id=1, source_target_pairs={{0,4},{2,6},{4,0},{6,2},{8,12},{10,14},{12,8},{14,10},{16,20},{18,... | collective-permute-start | bytes 3538952 | tf_op jit(solution)/shard_map/ppermute | solution.py:619
  179.0 56.1 %collective-permute-start.22 = (f32[512,768]{1,0:T(8,128)}, f32[512,768]{1,0:T(8,128)S(1)}, u32[]{:S(2)}, u32[]{:S(2)}) collective-permute-start(f32[512,768]{1,0:T(8,128)} %get-tuple-element.95), channel_id=1, source_target_pairs={{0,1},{1,0},{2,3},{3,2},{4,5},{5,4},{6,7},{7,6},{8,9},{9,8},{10,11... | collective-permute-start | bytes 4718600 | tf_op jit(solution)/shard_map/ppermute | solution.py:633
  187.5 53.6 %collective-permute-start.25 = (bf16[8,48,1536]{2,1,0:T(8,128)(2,1)}, bf16[8,48,1536]{2,1,0:T(8,128)(2,1)}, u32[]{:S(2)}, u32[]{:S(2)}) collective-permute-start(bf16[8,48,1536]{2,1,0:T(8,128)(2,1)} %get-tuple-element.101), channel_id=1, source_target_pairs={{0,2},{2,0},{4,6},{6,4},{8,10},{10,8},{12,14},{14,12},{16,18},{18,... | collective-permute-start | bytes 3538952 | tf_op jit(solution)/shard_map/ppermute | solution.py:619
  188.7 56.8 %collective-permute-start.27 = (bf16[8,48,1536]{2,1,0:T(8,128)(2,1)}, bf16[8,48,1536]{2,1,0:T(8,128)(2,1)S(1)}, u32[]{:S(2)}, u32[]{:S(2)}) collective-permute-start(bf16[8,48,1536]{2,1,0:T(8,128)(2,1)} %get-tuple-element.103), channel_id=1, source_target_pairs={{0,4},{2,6},{4,0},{6,2},{8,12},{10,14},{12,8},{14,10},{16,20},{18,... | collective-permute-start | bytes 3538952 | tf_op jit(solution)/shard_map/ppermute | solution.py:619
  211.3 37.2 %collective-permute-start.24 = (f32[512,768]{1,0:T(8,128)}, f32[512,768]{1,0:T(8,128)}, u32[]{:S(2)}, u32[]{:S(2)}) collective-permute-start(f32[512,768]{1,0:T(8,128)} %get-tuple-element.121.refs_1_), channel_id=1, source_target_pairs={{0,1},{1,0},{2,3},{3,2},{4,5},{5,4},{6,7},{7,6},{8,9},{9,8},{10,11... | collective-permute-start | bytes 4718600 | tf_op jit(solution)/shard_map/ppermute | solution.py:633
  220.3 18.0 %collective-permute-start.26 = (f32[256,768]{1,0:T(8,128)}, f32[256,768]{1,0:T(8,128)}, u32[]{:S(2)}, u32[]{:S(2)}) collective-permute-start(f32[256,768]{1,0:T(8,128)} %constant_dynamic-slice_fusion.26), channel_id=1, source_target_pairs={{0,1},{1,0},{2,3},{3,2},{4,5},{5,4},{6,7},{7,6},{8,9},{9,8},{10,11... | collective-permute-start | bytes 2359304 | tf_op jit(solution)/shard_map/ppermute | solution.py:633
  235.2 39.2 %collective-permute-start.44 = (bf16[8,48,768]{2,1,0:T(8,128)(2,1)}, bf16[8,48,768]{2,1,0:T(8,128)(2,1)}, u32[]{:S(2)}, u32[]{:S(2)}) collective-permute-start(bf16[8,48,768]{2,1,0:T(8,128)(2,1)} %get-tuple-element.118), channel_id=1, source_target_pairs={{0,4},{2,6},{4,0},{6,2},{8,12},{10,14},{12,8},{14,10},{16,20},{18,... | collective-permute-start | bytes 1769480 | tf_op jit(solution)/shard_map/ppermute | solution.py:619
  238.3 36.2 %collective-permute-start.43 = (bf16[8,48,768]{2,1,0:T(8,128)(2,1)}, bf16[8,48,768]{2,1,0:T(8,128)(2,1)}, u32[]{:S(2)}, u32[]{:S(2)}) collective-permute-start(bf16[8,48,768]{2,1,0:T(8,128)(2,1)} %get-tuple-element.116), channel_id=1, source_target_pairs={{0,2},{2,0},{4,6},{6,4},{8,10},{10,8},{12,14},{14,12},{16,18},{18,... | collective-permute-start | bytes 1769480 | tf_op jit(solution)/shard_map/ppermute | solution.py:619
  241.2 100.5 %collective-permute-start.31 = (bf16[256,768]{1,0:T(8,128)(2,1)}, bf16[256,768]{1,0:T(8,128)(2,1)}, u32[]{:S(2)}, u32[]{:S(2)}) collective-permute-start(bf16[256,768]{1,0:T(8,128)(2,1)} %add_convert_fusion.4), channel_id=1, source_target_pairs={{2,0},{4,2},{6,4},{8,6},{10,8},{12,10},{14,12},{16,14},{18,16},{20... | collective-permute-start | bytes 1179656 | tf_op jit(solution)/shard_map/ppermute | solution.py:625
  246.5 32.8 %collective-permute-start.49 = (bf16[2,2,48,1536]{3,2,0,1:T(8,128)(2,1)}, bf16[2,2,48,1536]{3,2,0,1:T(8,128)(2,1)}, u32[]{:S(2)}, u32[]{:S(2)}) collective-permute-start(bf16[2,2,48,1536]{3,2,0,1:T(8,128)(2,1)} %fusion.15), channel_id=1, source_target_pairs={{0,4},{2,6},{4,0},{6,2},{8,12},{10,14},{12,8},{14,10},{16,20},{18,... | collective-permute-start | bytes 1769480 | tf_op jit(solution)/shard_map/ppermute | solution.py:619
  248.6 38.2 %collective-permute-start.50 = (bf16[2,2,48,1536]{3,2,0,1:T(8,128)(2,1)S(1)}, bf16[2,2,48,1536]{3,2,0,1:T(8,128)(2,1)S(1)}, u32[]{:S(2)}, u32[]{:S(2)}) collective-permute-start(bf16[2,2,48,1536]{3,2,0,1:T(8,128)(2,1)S(1)} %fusion.16), channel_id=1, source_target_pairs={{0,2},{2,0},{4,6},{6,4},{8,10},{10,8},{12,14},{14,12},{16,18},{18,... | collective-permute-start | bytes 1769480 | tf_op jit(solution)/shard_map/ppermute | solution.py:619
  274.4 46.2 %collective-permute-start.38 = (bf16[8,48,768]{2,1,0:T(8,128)(2,1)}, bf16[8,48,768]{2,1,0:T(8,128)(2,1)}, u32[]{:S(2)}, u32[]{:S(2)}) collective-permute-start(bf16[8,48,768]{2,1,0:T(8,128)(2,1)} %get-tuple-element.134), channel_id=1, source_target_pairs={{0,4},{2,6},{4,0},{6,2},{8,12},{10,14},{12,8},{14,10},{16,20},{18,... | collective-permute-start | bytes 1769480 | tf_op jit(solution)/shard_map/ppermute | solution.py:619
  274.4 42.5 %collective-permute-start.37 = (bf16[8,48,768]{2,1,0:T(8,128)(2,1)}, bf16[8,48,768]{2,1,0:T(8,128)(2,1)}, u32[]{:S(2)}, u32[]{:S(2)}) collective-permute-start(bf16[8,48,768]{2,1,0:T(8,128)(2,1)} %get-tuple-element.132), channel_id=1, source_target_pairs={{0,2},{2,0},{4,6},{6,4},{8,10},{10,8},{12,14},{14,12},{16,18},{18,... | collective-permute-start | bytes 1769480 | tf_op jit(solution)/shard_map/ppermute | solution.py:619
  279.4 17.5 %collective-permute-start.45 = (bf16[2,2,48,768]{3,2,0,1:T(8,128)(2,1)}, bf16[2,2,48,768]{3,2,0,1:T(8,128)(2,1)}, u32[]{:S(2)}, u32[]{:S(2)}) collective-permute-start(bf16[2,2,48,768]{3,2,0,1:T(8,128)(2,1)} %fusion.33), channel_id=1, source_target_pairs={{0,4},{2,6},{4,0},{6,2},{8,12},{10,14},{12,8},{14,10},{16,20},{18,... | collective-permute-start | bytes 884744 | tf_op jit(solution)/shard_map/ppermute | solution.py:619
  316.3 21.6 %collective-permute-start.28 = (f32[256,768]{1,0:T(8,128)S(1)}, f32[256,768]{1,0:T(8,128)S(1)}, u32[]{:S(2)}, u32[]{:S(2)}) collective-permute-start(f32[256,768]{1,0:T(8,128)S(1)} %constant_dynamic-slice_fusion.18), channel_id=1, source_target_pairs={{0,1},{1,0},{2,3},{3,2},{4,5},{5,4},{6,7},{7,6},{8,9},{9,8},{10,11... | collective-permute-start | bytes 2359304 | tf_op jit(solution)/shard_map/ppermute | solution.py:633
  316.9 18.9 %collective-permute-start.51 = (bf16[2,48,3072]{2,1,0:T(8,128)(2,1)S(1)}, bf16[2,48,3072]{2,1,0:T(8,128)(2,1)S(1)}, u32[]{:S(2)}, u32[]{:S(2)}) collective-permute-start(bf16[2,48,3072]{2,1,0:T(8,128)(2,1)S(1)} %copy-done.27), channel_id=1, source_target_pairs={{0,8},{2,10},{4,12},{6,14},{8,0},{10,2},{12,4},{14,6},{16,24},{18,... | collective-permute-start | bytes 1769480 | tf_op jit(solution)/shard_map/ppermute | solution.py:619
  316.9 19.3 %collective-permute-start.48 = (bf16[48,1536]{1,0:T(8,128)(2,1)S(1)}, bf16[48,1536]{1,0:T(8,128)(2,1)S(1)}, u32[]{:S(2)}, u32[]{:S(2)}) collective-permute-start(bf16[48,1536]{1,0:T(8,128)(2,1)S(1)} %fusion.45), channel_id=1, source_target_pairs={{0,16},{2,18},{4,20},{6,22},{8,24},{10,26},{12,28},{14,30},{16,0},... | collective-permute-start | bytes 442376 | tf_op jit(solution)/shard_map/ppermute | solution.py:619
  320.7 23.7 %collective-permute-start.39 = (bf16[2,2,48,768]{3,2,0,1:T(8,128)(2,1)S(1)}, bf16[2,2,48,768]{3,2,0,1:T(8,128)(2,1)S(1)}, u32[]{:S(2)}, u32[]{:S(2)}) collective-permute-start(bf16[2,2,48,768]{3,2,0,1:T(8,128)(2,1)S(1)} %fusion.31), channel_id=1, source_target_pairs={{0,4},{2,6},{4,0},{6,2},{8,12},{10,14},{12,8},{14,10},{16,20},{18,... | collective-permute-start | bytes 884744 | tf_op jit(solution)/shard_map/ppermute | solution.py:619
  336.2 18.6 %collective-permute-start.52 = (bf16[48,3072]{1,0:T(8,128)(2,1)S(1)}, bf16[48,3072]{1,0:T(8,128)(2,1)S(1)}, u32[]{:S(2)}, u32[]{:S(2)}) collective-permute-start(bf16[48,3072]{1,0:T(8,128)(2,1)S(1)} %fusion.35), channel_id=1, source_target_pairs={{0,16},{2,18},{4,20},{6,22},{8,24},{10,26},{12,28},{14,30},{16,0},... | collective-permute-start | bytes 884744 | tf_op jit(solution)/shard_map/ppermute | solution.py:619
  344.3 39.3 %collective-permute-start.32 = (f32[512,768]{1,0:T(8,128)}, f32[512,768]{1,0:T(8,128)}, u32[]{:S(2)}, u32[]{:S(2)}) collective-permute-start(f32[512,768]{1,0:T(8,128)} %maximum_add_fusion.1), channel_id=1, source_target_pairs={{0,1},{1,0},{2,3},{3,2},{4,5},{5,4},{6,7},{7,6},{8,9},{9,8},{10,11... | collective-permute-start | bytes 4718600 | tf_op jit(solution)/shard_map/ppermute | solution.py:633
  (71 other events, 493.0 us)
